TPU v7x, 256 devices: a whole 4x4x8 slice. The times are simulated.
256 devices in a mesh: lat: 16 (over y, x_hi, core), lon: 16 (over z, x_lo).
Axes of the slice: x: 4 (x_hi: 2, x_lo: 2; x = x_hi * 2 + x_lo), y: 4, z: 8, core: 2. Of those that a mesh axis runs over, the one named last changes fastest.
Arguments:
- potential_heat_state: float32 [16, 1024, 2048], P(None, 'lat', 'lon'), may hold values from -6 to 6
- saltiness_anomaly: float32 [16, 1024, 2048], P(None, 'lat', 'lon'), may hold values from -6 to 6
- first_current_component: float32 [16, 1024, 2048], P(None, 'lat', 'lon'), may hold values from -6 to 6
- second_current_component: float32 [16, 1024, 2048], P(None, 'lat', 'lon'), may hold values from -6 to 6
- bathymetry_layer_total: int32 [1024, 2048], P('lat', 'lon'), may hold values from 0 to 16
- westeast_cell_extent: float32 [1024, 2048], P('lat', 'lon'), may hold values from 1 to 2
- southnorth_cell_extent: float32 [1024, 2048], P('lat', 'lon'), may hold values from 1 to 2
- planetary_vorticity: float32 [1024, 2048], P('lat', 'lon'), may hold values from -1.5 to 1.5
- scalar_mixing_factor: float32 [16], replicated, may hold values from 0.05 to 0.5
- momentum_mixing_factor: float32 [16], replicated, may hold values from 0.05 to 0.5
Outputs:
- new_temperature: float32 [16, 1024, 2048], P(None, 'lat', 'lon')
- new_salinity: float32 [16, 1024, 2048], P(None, 'lat', 'lon')
- new_zonal: float32 [16, 1024, 2048], P(None, 'lat', 'lon')
- new_north: float32 [16, 1024, 2048], P(None, 'lat', 'lon')
All inputs are finite; a program needn't handle non-finite values.
Results may differ from a plain program's by a relative error of at most 0.00002.
Values sent between devices are 32-bit elements; how exact they have to be, the bound alone decides.
No kernel may reach another device: no remote copies, remote signals or barrier semaphores. Data moves between devices by JAX's collectives and lax.ppermute only.
A program may use at most 64 MiB of HBM per device.

v0:
```python
import jax
import jax.numpy as jnp
from jax import lax
from jax.experimental import pallas as pl
from jax.experimental.pallas import tpu as pltpu
from jax.sharding import PartitionSpec as P


STEPS = 3
NF = 4
NK = 16
NR = 64
NC = 128
HALO = 3
MSG = 208
GH = 216
SR = 88
OFF = 10
NT = 9

F32 = jnp.float32
VM = pl.BlockSpec(memory_space=pltpu.VMEM)
SM = pl.BlockSpec(memory_space=pltpu.SMEM)
HB = pl.BlockSpec(memory_space=pl.ANY)


def params(mib):
    return pltpu.CompilerParams(vmem_limit_bytes=mib * 2**20)


def lanes():
    return lax.broadcasted_iota(jnp.int32, (8, NC), 1)


def pick(x, index):
    return jnp.take_along_axis(x, index, axis=1, mode="promise_in_bounds")


def metric(wd, ht, cor):
    iw, ih = 1.0 / wd, 1.0 / ht
    return 0.1 * iw, 0.1 * ih, 0.2 * (iw * iw), 0.2 * (ih * ih), 0.2 * cor


def advance(c, e, w, n, s, co, wet, mix):
    a1, b1, a2, b2, f2 = co
    p, r = a1 * c[2], b1 * c[3]
    out = []
    for pair, d in ((0, mix[0]), (2, mix[1])):
        ax, by = d * a2, d * b2
        ce, cw, cn, cs = ax - p, ax + p, by - r, by + r
        cc = 1.0 - 2.0 * (ax + by)
        for q in (pair, pair + 1):
            v = (ce * e[q] + cw * w[q]) + (cn * n[q] + cs * s[q]) + cc * c[q]
            if q == 2:
                v = v + f2 * c[3]
            if q == 3:
                v = v - f2 * c[2]
            out.append(jnp.where(wet, v, 0.0))
    return out


def pack_rows(t, s, u, v, bat, wd, ht, cor, m1, m2, buf, pbuf, ibuf, sems, psems):
    lat = lax.axis_index("lat")
    last = lax.axis_size("lat") - 1
    fields = (t, s, u, v)
    copies = []
    for side, r0 in ((0, 0), (1, NR - 8)):
        for q in range(NF):
            copies.append(
                pltpu.make_async_copy(
                    fields[q].at[:, pl.ds(r0, 8), :], buf.at[q, side], sems.at[2 * q + side]
                )
            )
        for q, ref in enumerate((wd, ht, cor)):
            copies.append(
                pltpu.make_async_copy(
                    ref.at[pl.ds(r0, 8), :], pbuf.at[q, side], psems.at[2 * q + side]
                )
            )
        copies.append(
            pltpu.make_async_copy(bat.at[pl.ds(r0, 8), :], ibuf.at[side], psems.at[6 + side])
        )
    for c in copies:
        c.start()
    zero = jnp.zeros((8, NC), F32)
    m1[MSG - 8 : MSG, :] = zero
    m2[MSG - 8 : MSG, :] = zero
    for c in copies:
        c.wait()
    pbuf[3, 0] = ibuf[0].astype(F32)
    pbuf[3, 1] = ibuf[1].astype(F32)
    base = NF * NK * HALO

    def plain(dst, side):
        r0 = 0 if side == 0 else 8 - HALO
        for q in range(NF):
            for k in range(NK):
                i = (q * NK + k) * HALO
                dst[i : i + HALO, :] = buf[q, side, k, r0 : r0 + HALO, :]
        for q in range(4):
            i = base + q * HALO
            dst[i : i + HALO, :] = pbuf[q, side, r0 : r0 + HALO, :]

    def folded(dst):
        back = NC - 1 - lanes()
        for q in range(NF):
            for k in range(NK):
                x = pick(buf[q, 1, k], back)
                x = -x if q >= 2 else x
                i = (q * NK + k) * HALO
                for m in range(HALO):
                    dst[i + m : i + m + 1, :] = x[7 - m : 8 - m, :]
        for q in range(4):
            x = pick(pbuf[q, 1], back)
            i = base + q * HALO
            for m in range(HALO):
                dst[i + m : i + m + 1, :] = x[7 - m : 8 - m, :]

    odd = lax.rem(lat, 2) == 1

    @pl.when(jnp.logical_not(odd))
    def _():
        plain(m2, 0)
        plain(m1, 1)

    @pl.when(odd)
    def _():
        plain(m1, 0)

    @pl.when(jnp.logical_and(odd, lat != last))
    def _():
        plain(m2, 1)

    @pl.when(lat == last)
    def _():
        folded(m2)


def interior(levels, fields, bat, mt, ms, co, a, b, out):
    def level(k, carry):
        mix = (mt[k], ms[k])
        for j in range(8):
            wet = k < bat[8 * j : 8 * j + 8, :]
            for q in range(NF):
                a[q, 8 + 8 * j : 16 + 8 * j, :] = jnp.where(
                    wet, fields[q][k, 8 * j : 8 * j + 8, :], 0.0
                )
        src, dst = a, b
        for step in range(STEPS):
            for j in range(8):
                r = 8 + 8 * j
                wet = k < bat[8 * j : 8 * j + 8, :]
                c = [src[q, r : r + 8, :] for q in range(NF)]
                n = [src[q, r + 1 : r + 9, :] for q in range(NF)]
                s = [src[q, r - 1 : r + 7, :] for q in range(NF)]
                e = [pltpu.roll(x, NC - 1, 1) for x in c]
                w = [pltpu.roll(x, 1, 1) for x in c]
                cs = [co[i, 8 * j : 8 * j + 8, :] for i in range(5)]
                new = advance(c, e, w, n, s, cs, wet, mix)
                for q in range(NF):
                    if step == STEPS - 1:
                        out[q, k, 8 * j : 8 * j + 8, :] = new[q]
                    else:
                        dst[q, r : r + 8, :] = new[q]
            src, dst = dst, src
        return carry

    lax.fori_loop(levels[0], levels[1], level, 0)


def set_metric(co, wd, ht, cor):
    for j in range(8):
        rows = slice(8 * j, 8 * j + 8)
        for i, x in enumerate(metric(wd[rows, :], ht[rows, :], cor[rows, :])):
            co[i, rows, :] = x


def strip_index():
    lane = lanes()
    block, level = lane // NK, lane % NK
    west = jnp.where(block >= HALO, block - HALO, NC - 6)
    east = jnp.where(block < 5, block + NC - 5, 5)
    return level, west, east


def zero_rims(a, b):
    zero = jnp.zeros((8, NC), F32)
    for q in range(NF):
        for x in (a, b):
            x[q, 0:8, :] = zero
            x[q, NR + 8 : NR + 16, :] = zero


def inside_kernel(levels, mt, ms, t, s, u, v, bat, wd, ht, cor, out, gw, ge, pw, pe, a, b, co):
    fields = (t, s, u, v)
    level, west, east = strip_index()
    for j in range(8):
        rows = slice(8 * j, 8 * j + 8)
        for q in range(NF):
            xw = xe = jnp.zeros((8, NC), F32)
            for k in range(NK):
                x = fields[q][k, rows, :]
                here = level == k
                xw = jnp.where(here, pick(x, west), xw)
                xe = jnp.where(here, pick(x, east), xe)
            gw[q, rows, :] = xw
            ge[q, rows, :] = xe
        for i, ref in enumerate((wd, ht, cor, bat)):
            x = ref[rows, :].astype(F32)
            pw[i, rows, :] = pick(x, west)
            pe[i, rows, :] = pick(x, east)
    set_metric(co, wd, ht, cor)
    zero_rims(a, b)
    interior(levels, fields, bat, mt, ms, co, a, b, out)


def pack_columns(r1, r2, gw, ge, pw, pe, q1, q2, gh, sw, se, spw, spe):
    odd = lax.rem(lax.axis_index("lat"), 2) == 1
    even_lon = lax.rem(lax.axis_index("lon"), 2) == 0
    for i in range(MSG // 8):
        rows = slice(8 * i, 8 * i + 8)
        x1, x2 = r1[rows, :], r2[rows, :]
        gh[0, rows, :] = jnp.where(odd, x1, x2)
        gh[1, rows, :] = jnp.where(odd, x2, x1)
    zero = jnp.zeros((8, NC), F32)
    gh[0, MSG:GH, :] = zero
    gh[1, MSG:GH, :] = zero
    level, west, east = strip_index()
    for own, strip in ((gw, sw), (ge, se), (pw, spw), (pe, spe)):
        for q in range(4):
            strip[q, 0:8, :] = zero
            strip[q, 72:80, :] = zero
            strip[q, 80:88, :] = zero
            for j in range(8):
                strip[q, OFF + 8 * j : OFF + 8 * j + 8, :] = own[q, 8 * j : 8 * j + 8, :]
    for side, at in ((0, OFF - HALO), (1, OFF + NR)):
        for q in range(NF):
            xw = xe = zero
            for k in range(NK):
                i = (q * NK + k) * HALO
                x = gh[side, i : i + 8, :]
                here = level == k
                xw = jnp.where(here, pick(x, west), xw)
                xe = jnp.where(here, pick(x, east), xe)
            sw[q, at : at + HALO, :] = xw[:HALO, :]
            se[q, at : at + HALO, :] = xe[:HALO, :]
            i = NF * NK * HALO + q * HALO
            x = gh[side, i : i + 8, :]
            spw[q, at : at + HALO, :] = pick(x, west)[:HALO, :]
            spe[q, at : at + HALO, :] = pick(x, east)[:HALO, :]
    lane = lanes()
    first, second = lane < 48, lane < 96
    plane, column = (lane - 96) // HALO, lax.rem(jnp.maximum(lane - 96, 0), HALO)

    def emit(dst_e, dst_w):
        for dst, strip, planes, block in ((dst_e, se, spe, 2), (dst_w, sw, spw, 3)):
            start = block * NK
            which = (block + column) * NK
            for i in range(NT):
                rows = slice(OFF - HALO + 8 * i, OFF - HALO + 8 * i + 8)
                for pair in (0, 1):
                    x = strip[2 * pair, rows, :]
                    y = strip[2 * pair + 1, rows, :]
                    x = pltpu.roll(x, NC - start, 1)
                    if start != 48:
                        y = pltpu.roll(y, 48 - start, 1)
                    z = jnp.where(first, x, y)
                    if pair == 0:
                        for m in range(4):
                            take = jnp.logical_and(plane == m, jnp.logical_not(second))
                            z = jnp.where(take, pick(planes[m, rows, :], which), z)
                    dst[pair * 8 * NT + 8 * i : pair * 8 * NT + 8 * i + 8, :] = z

    @pl.when(even_lon)
    def _():
        emit(q1, q2)

    @pl.when(jnp.logical_not(even_lon))
    def _():
        emit(q2, q1)


def edge_rows(mt, ms, t, s, u, v, bat, wd, ht, cor, gh, out, win, pwin):
    fields = (t, s, u, v)
    base = NF * NK * HALO
    own = ((0, 10), (NR - 8, 6))
    ghost = (7, 14)
    co, wets, gwets = [], [], []
    for side in (0, 1):
        r0, at = own[side]
        g = ghost[side]
        for i, ref in enumerate((wd, ht, cor, bat)):
            pwin[side, i, at : at + 8, :] = ref[r0 : r0 + 8, :].astype(F32)
            pwin[side, i, g : g + HALO, :] = gh[side, base + i * HALO : base + (i + 1) * HALO, :]
        co.append(metric(*[pwin[side, i, 8:16, :] for i in range(3)]))
        wets.append(pwin[side, 3, 8:16, :])
        gwets.append(gh[side, base + 3 * HALO : base + 4 * HALO, :])
    group = 2

    def body(i, carry):
        work = []
        for g in range(group):
            k = i * group + g
            kf = k.astype(F32)
            for side in (0, 1):
                r0, at = own[side]
                gr = ghost[side]
                wet_own = k < bat[r0 : r0 + 8, :]
                wet_ghost = kf < gwets[side]
                for q in range(NF):
                    win[g, side, q, at : at + 8, :] = jnp.where(
                        wet_own, fields[q][k, r0 : r0 + 8, :], 0.0
                    )
                    x = gh[side, pl.ds((q * NK + k) * HALO, HALO), :]
                    win[g, side, q, gr : gr + HALO, :] = jnp.where(wet_ghost, x, 0.0)
                work.append((g, side, k, kf))
        state = []
        for g, side, k, kf in work:
            c = [win[g, side, q, 8:16, :] for q in range(NF)]
            n = [win[g, side, q, 9:17, :] for q in range(NF)]
            s_ = [win[g, side, q, 7:15, :] for q in range(NF)]
            state.append((c, n, s_))
        for step in range(STEPS):
            nxt = []
            for (g, side, k, kf), (c, n, s_) in zip(work, state):
                e = [pltpu.roll(x, NC - 1, 1) for x in c]
                w = [pltpu.roll(x, 1, 1) for x in c]
                c = advance(c, e, w, n, s_, co[side], kf < wets[side], (mt[k], ms[k]))
                n = s_ = None
                if step < STEPS - 1:
                    n = [pltpu.roll(x, 7, 0) for x in c]
                    s_ = [pltpu.roll(x, 1, 0) for x in c]
                nxt.append((c, n, s_))
            state = nxt
        for (g, side, k, kf), (c, _, _) in zip(work, state):
            for q in range(NF):
                out[side, q, k, :, :] = pltpu.roll(c[q], 6 if side == 0 else 2, 0)
        return carry

    lax.fori_loop(0, NK // group, body, 0)


def edge_kernel(levels, mt, ms, t, s, u, v, bat, wd, ht, cor, gh, out, more, win, pwin, a, b, co):
    edge_rows(mt, ms, t, s, u, v, bat, wd, ht, cor, gh, out, win, pwin)
    if levels[0] < levels[1]:
        set_metric(co, wd, ht, cor)
        zero_rims(a, b)
        interior(levels, (t, s, u, v), bat, mt, ms, co, a, b, more)


def finish(
    split, mt, ms, q1, q2, gw, ge, sw, se, spw, spe, rows_new, inner, inner2,
    ot, os, ou, ov, aw, ae, bw, be, cw, ce, zed, res, sems,
):
    even = lax.rem(lax.axis_index("lon"), 2) == 0
    lane = lanes()
    block, level = lane // NK, lane % NK
    dt = du = jnp.zeros((8, NC), F32)
    for k in range(NK):
        here = level == k
        dt = jnp.where(here, mt[k], dt)
        du = jnp.where(here, ms[k], du)
    level_f = level.astype(F32)
    zero = jnp.zeros((8, NC), F32)
    sides = (
        (0, aw, bw, cw, sw, spw, block < HALO, block, (0, 80)),
        (1, ae, be, ce, se, spe, block >= 5, block - 5, (80, 32)),
    )
    for side, a, b, co, strip, planes, from_ghost, column, shifts in sides:
        which = 96 + jnp.clip(column, 0, HALO - 1)
        for x in (a, b):
            for q in range(NF):
                x[q, 0:8, :] = zero
                x[q, 80:88, :] = zero
        for q in range(NF):
            co[5, 0:8, :] = zero
        for i in range(NT):
            rows = slice(OFF - HALO + 8 * i, OFF - HALO + 8 * i + 8)
            g = []
            for pair in (0, 1):
                at = slice(pair * 8 * NT + 8 * i, pair * 8 * NT + 8 * i + 8)
                x1, x2 = q1[at, :], q2[at, :]
                g.append(
                    jnp.where(even, x2, x1) if side == 0 else jnp.where(even, x1, x2)
                )
            pls = []
            for m in range(4):
                pls.append(
                    jnp.where(from_ghost, pick(g[0], which + m * HALO), planes[m, rows, :])
                )
            for m, x in enumerate(metric(*pls[:3])):
                co[m, rows, :] = x
            co[5, rows, :] = pls[3]
            wet = level_f < pls[3]
            for q in range(NF):
                sh = shifts[q % 2]
                x = g[q // 2] if sh == 0 else pltpu.roll(g[q // 2], sh, 1)
                x = jnp.where(from_ghost, x, strip[q, rows, :])
                a[q, rows, :] = jnp.where(wet, x, 0.0)
    extra_w, extra_e = block == 7, block == 0
    for step in range(STEPS):
        for i in range(NT):
            r = 8 + 8 * i
            for side, a, b, co, strip, planes, from_ghost, column, shifts in sides:
                src, dst = (a, b) if step % 2 == 0 else (b, a)
                c = [src[q, r : r + 8, :] for q in range(NF)]
                n = [src[q, r + 1 : r + 9, :] for q in range(NF)]
                s = [src[q, r - 1 : r + 7, :] for q in range(NF)]
                e = [pltpu.roll(x, NC - NK, 1) for x in c]
                w = [pltpu.roll(x, NK, 1) for x in c]
                if step == 0:
                    if side == 0:
                        wet = level_f < spe[3, r : r + 8, :]
                        e = [
                            jnp.where(extra_w, jnp.where(wet, se[q, r : r + 8, :], 0.0), e[q])
                            for q in range(NF)
                        ]
                    else:
                        wet = level_f < spw[3, r : r + 8, :]
                        w = [
                            jnp.where(extra_e, jnp.where(wet, sw[q, r : r + 8, :], 0.0), w[q])
                            for q in range(NF)
                        ]
                cs = [co[m, r : r + 8, :] for m in range(5)]
                new = advance(c, e, w, n, s, cs, level_f < co[5, r : r + 8, :], (dt, du))
                for q in range(NF):
                    dst[q, r : r + 8, :] = new[q]
    fin_w, fin_e = (bw, be) if STEPS % 2 else (aw, ae)
    middle = jnp.logical_and(lane >= 48, lane < 96)
    for q in range(NF):
        for j in range(8):
            rows = slice(OFF + 8 * j, OFF + 8 * j + 8)
            zed[q, 8 * j : 8 * j + 8, :] = jnp.where(
                middle, fin_w[q, rows, :], pltpu.roll(fin_e[q, rows, :], 64, 1)
            )
    low, high = lane < HALO, lane >= NC - HALO
    edge = jnp.logical_or(low, high)
    where_from = jnp.where(
        low, (lane + HALO) * NK, jnp.where(high, lax.rem((lane - 119) * NK, NC), 0)
    )
    row = lax.broadcasted_iota(jnp.int32, (8, NC), 0)
    top, bottom = row < HALO, row >= 8 - HALO
    outs = (ot, os, ou, ov)

    def level_out(src, k):
        index = where_from + k
        for q in range(NF):
            for j in range(8):
                rows = slice(8 * j, 8 * j + 8)
                x = src[q, k, rows, :]
                if j == 0:
                    x = jnp.where(top, rows_new[0, q, k, :, :], x)
                if j == 7:
                    x = jnp.where(bottom, rows_new[1, q, k, :, :], x)
                res[q, k, rows, :] = jnp.where(edge, pick(zed[q, rows, :], index), x)

    group = 4

    def copy(q, g):
        return pltpu.make_async_copy(
            res.at[q, pl.ds(g * group, group)], outs[q].at[pl.ds(g * group, group)], sems.at[q, g]
        )

    for g in range(NK // group):
        for lo, hi, src in ((0, split, inner), (split, NK, inner2)):
            lo, hi = max(lo, g * group), min(hi, (g + 1) * group)
            if lo < hi:
                lax.fori_loop(lo, hi, lambda k, c, src=src: (level_out(src, k), c)[1], 0)
        for q in range(NF):
            copy(q, g).start()
    for g in range(NK // group):
        for q in range(NF):
            copy(q, g).wait()


def row_pairs(nl, no):
    near, far = [], []
    for j in range(nl):
        for i in range(no):
            near.append((j * no + i, (j ^ 1) * no + i))
            if j == nl - 1:
                far.append((j * no + i, j * no + no - 1 - i))
            elif j % 2:
                far.append((j * no + i, (j + 1) * no + i))
            elif j > 0:
                far.append((j * no + i, (j - 1) * no + i))
    return near, far


def column_pairs(nl, no):
    near, far = [], []
    for j in range(nl):
        for i in range(no):
            near.append((j * no + i, j * no + (i ^ 1)))
            far.append((j * no + i, j * no + ((i + 1) % no if i % 2 else (i - 1) % no)))
    return near, far


SPLIT = 16


def on_device(t, s, u, v, bat, wd, ht, cor, mt, ms):
    nl, no = lax.axis_size("lat"), lax.axis_size("lon")
    axes = ("lat", "lon")
    sds = lambda *shape: jax.ShapeDtypeStruct(shape, F32)
    vm = lambda *shape: pltpu.VMEM(shape, F32)
    cost = lambda us: pl.CostEstimate(
        flops=int(us * 1e6), bytes_accessed=int(us * 3e6), transcendentals=0
    )
    m1, m2 = pl.pallas_call(
        pack_rows,
        out_shape=(sds(MSG, NC), sds(MSG, NC)),
        in_specs=[HB] * 8,
        out_specs=(VM, VM),
        scratch_shapes=[
            vm(NF, 2, NK, 8, NC),
            vm(4, 2, 8, NC),
            pltpu.VMEM((2, 8, NC), jnp.int32),
            pltpu.SemaphoreType.DMA((8,)),
            pltpu.SemaphoreType.DMA((8,)),
        ],
        compiler_params=params(4),
        cost_estimate=cost(1),
        name="pack_rows",
    )(t, s, u, v, bat, wd, ht, cor)
    near, far = row_pairs(nl, no)
    r2 = lax.ppermute(m2, axes, far)
    r1 = lax.ppermute(m1, axes, near)
    inner, gw, ge, pw, pe = pl.pallas_call(
        lambda *refs: inside_kernel((0, SPLIT), *refs),
        out_shape=(sds(NF, SPLIT, NR, NC),) + (sds(4, NR, NC),) * 4,
        in_specs=[SM, SM] + [VM] * 8,
        out_specs=(VM,) * 5,
        scratch_shapes=[vm(NF, 80, NC), vm(NF, 80, NC), vm(5, NR, NC)],
        compiler_params=params(4),
        cost_estimate=cost(4),
        name="inside",
    )(mt, ms, t, s, u, v, bat, wd, ht, cor)
    q1, q2, gh, sw, se, spw, spe = pl.pallas_call(
        pack_columns,
        out_shape=(sds(16 * NT, NC),) * 2 + (sds(2, GH, NC),) + (sds(4, SR, NC),) * 4,
        in_specs=[VM] * 6,
        out_specs=(VM,) * 7,
        compiler_params=params(4),
        cost_estimate=cost(1),
        name="pack_columns",
    )(r1, r2, gw, ge, pw, pe)
    near, far = column_pairs(nl, no)
    p2 = lax.ppermute(q2, axes, far)
    p1 = lax.ppermute(q1, axes, near)
    rows_new, inner2 = pl.pallas_call(
        lambda *refs: edge_kernel((SPLIT, NK), *refs),
        out_shape=(sds(2, NF, NK, 8, NC), sds(NF, NK, NR, NC) if SPLIT < NK else sds(8, NC)),
        in_specs=[SM, SM] + [VM] * 9,
        out_specs=(VM,) * 2,
        scratch_shapes=[
            vm(2, 2, NF, 24, NC),
            vm(2, 4, 24, NC),
            vm(NF, 80, NC),
            vm(NF, 80, NC),
            vm(5, NR, NC),
        ],
        compiler_params=params(4),
        cost_estimate=cost(2),
        name="edge_rows",
    )(mt, ms, t, s, u, v, bat, wd, ht, cor, gh)
    return pl.pallas_call(
        lambda *refs: finish(SPLIT, *refs),
        out_shape=(sds(NK, NR, NC),) * 4,
        in_specs=[SM, SM] + [VM] * 11,
        out_specs=(HB,) * 4,
        scratch_shapes=[vm(NF, SR, NC)] * 4
        + [vm(6, SR, NC)] * 2
        + [vm(NF, NR, NC), vm(NF, NK, NR, NC), pltpu.SemaphoreType.DMA((NF, 4))],
        compiler_params=params(8),
        cost_estimate=cost(2),
        name="finish",
    )(mt, ms, p1, p2, gw, ge, sw, se, spw, spe, rows_new, inner, inner2)


def solution(mesh):
    block = P(None, "lat", "lon")
    plane = P("lat", "lon")
    return jax.shard_map(
        on_device,
        mesh=mesh,
        in_specs=(block,) * 4 + (plane,) * 4 + (P(), P()),
        out_specs=(block,) * 4,
        check_vma=False,
    )
```

profile of v0, /device:TPU:1, one launch (start us, length us, event | category | flops | bytes accessed | tf_op | source)
XLA Modules:
  0.0 36.1 jit_solution(5020169620638159037)
XLA Ops:
  0.6 1.0 %copy-done = f32[16,64,128]{2,1,0:T(8,128)S(1)} copy-done((f32[16,64,128]{2,1,0:T(8,128)S(1)}, f32[16,64,128]{2,1,0:T(8,128)}, u32[]{:S(2)}) %copy-start) | copy-done | bytes 524312
  1.7 1.0 %copy-done.2 = f32[16,64,128]{2,1,0:T(8,128)S(1)} copy-done((f32[16,64,128]{2,1,0:T(8,128)S(1)}, f32[16,64,128]{2,1,0:T(8,128)}, u32[]{:S(2)}) %copy-start.2) | copy-done | bytes 524312
  2.7 1.0 %copy-done.4 = f32[16,64,128]{2,1,0:T(8,128)S(1)} copy-done((f32[16,64,128]{2,1,0:T(8,128)S(1)}, f32[16,64,128]{2,1,0:T(8,128)}, u32[]{:S(2)}) %copy-start.4) | copy-done | bytes 524312
  3.8 1.0 %copy-done.6 = f32[16,64,128]{2,1,0:T(8,128)S(1)} copy-done((f32[16,64,128]{2,1,0:T(8,128)S(1)}, f32[16,64,128]{2,1,0:T(8,128)}, u32[]{:S(2)}) %copy-start.6) | copy-done | bytes 524312
  4.8 0.8 %copy-done.8 = s32[64,128]{1,0:T(8,128)S(1)} copy-done((s32[64,128]{1,0:T(8,128)S(1)}, s32[64,128]{1,0:T(8,128)}, u32[]{:S(2)}) %copy-start.8) | copy-done | bytes 32792
  5.6 0.8 %copy-done.9 = f32[64,128]{1,0:T(8,128)S(1)} copy-done((f32[64,128]{1,0:T(8,128)S(1)}, f32[64,128]{1,0:T(8,128)}, u32[]{:S(2)}) %copy-start.9) | copy-done | bytes 32792
  6.3 0.8 %copy-done.10 = f32[64,128]{1,0:T(8,128)S(1)} copy-done((f32[64,128]{1,0:T(8,128)S(1)}, f32[64,128]{1,0:T(8,128)}, u32[]{:S(2)}) %copy-start.10) | copy-done | bytes 32792
  7.1 0.8 %copy-done.11 = f32[64,128]{1,0:T(8,128)S(1)} copy-done((f32[64,128]{1,0:T(8,128)S(1)}, f32[64,128]{1,0:T(8,128)}, u32[]{:S(2)}) %copy-start.11) | copy-done | bytes 32792
  7.8 0.0 copy-start.5
  7.9 0.0 copy-start.7
  7.9 0.4 pack_rows.1
  8.2 3.3 %collective-permute-start = (f32[208,128]{1,0:T(8,128)S(1)}, f32[208,128]{1,0:T(8,128)S(1)}, u32[]{:S(2)}, u32[]{:S(2)}) collective-permute-start(f32[208,128]{1,0:T(8,128)S(1)} %get-tuple-element.20), channel_id=1, source_target_pairs={{0,16},{1,17},{2,18},{3,19},{4,20},{5,21},{6,22},{7,23},{8,24},{9,... | collective-permute-start | bytes 319496 | tf_op jit(solution)/shard_map/ppermute | solution.py:528
  11.6 2.9 %collective-permute-start.1 = (f32[208,128]{1,0:T(8,128)S(1)}, f32[208,128]{1,0:T(8,128)S(1)}, u32[]{:S(2)}, u32[]{:S(2)}) collective-permute-start(f32[208,128]{1,0:T(8,128)S(1)} %get-tuple-element.21), channel_id=1, source_target_pairs={{16,32},{17,33},{18,34},{19,35},{20,36},{21,37},{22,38},{23,39},{2... | collective-permute-start | bytes 319496 | tf_op jit(solution)/shard_map/ppermute | solution.py:527
  14.5 0.0 copy-done.12
  14.5 6.9 %inside.1 = (f32[4,16,64,128]{3,2,1,0:T(8,128)S(1)}, f32[4,64,128]{2,1,0:T(8,128)S(1)}, f32[4,64,128]{2,1,0:T(8,128)S(1)}, f32[4,64,128]{2,1,0:T(8,128)S(1)}, f32[4,64,128]{2,1,0:T(8,128)S(1)}) custom-call(f32[16]{0:T(128)S(1)} %copy-done.12, f32[16]{0:T(128)S(1)} %copy-done.13, f32[16,64,128]{2,1,0:T(8,128)S(1)} %copy-done, f32[16,64,128]{2,1,0:T(8,128)S(1)} %copy-done.2, ...), custom_call_target="tpu_custom_call" | custom-call | flops 4000000 | bytes 12000000 | tf_op jit(solution)/shard_map/inside/pallas_call | solution.py:529
  21.5 0.0 collective-permute-done.r1
  21.5 0.0 collective-permute-done.1.r2
  21.5 0.6 %pack_columns.1 = (f32[144,128]{1,0:T(8,128)S(1)}, f32[144,128]{1,0:T(8,128)S(1)}, f32[2,216,128]{2,1,0:T(8,128)S(1)}, f32[4,88,128]{2,1,0:T(8,128)S(1)}, f32[4,...) custom-call(f32[208,128]{1,0:T(8,128)S(1)} %collective-permute-done.r1, ...), custom_call_target="tpu_custom_call" | custom-call | flops 1000000 | bytes 3000000 | tf_op jit(solution)/shard_map/pack_columns/pallas_call | solution.py:539
  22.1 0.4 %collective-permute-start.2 = (f32[144,128]{1,0:T(8,128)S(1)}, f32[144,128]{1,0:T(8,128)S(1)}, u32[]{:S(2)}, u32[]{:S(2)}) collective-permute-start(f32[144,128]{1,0:T(8,128)S(1)} %get-tuple-element.26), channel_id=1, source_target_pairs={{0,1},{1,0},{2,3},{3,2},{4,5},{5,4},{6,7},{7,6},{8,9},{9,8},{10,11... | collective-permute-start | bytes 221192 | tf_op jit(solution)/shard_map/ppermute | solution.py:550
  22.5 6.4 %collective-permute-start.3 = (f32[144,128]{1,0:T(8,128)S(1)}, f32[144,128]{1,0:T(8,128)S(1)}, u32[]{:S(2)}, u32[]{:S(2)}) collective-permute-start(f32[144,128]{1,0:T(8,128)S(1)} %get-tuple-element.27), channel_id=1, source_target_pairs={{0,15},{1,2},{2,1},{3,4},{4,3},{5,6},{6,5},{7,8},{8,7},{9,10},{10,... | collective-permute-start | bytes 221192 | tf_op jit(solution)/shard_map/ppermute | solution.py:549
  29.0 3.0 %edge_rows.1 = (f32[2,4,16,8,128]{4,3,2,1,0:T(8,128)S(1)}, f32[8,128]{1,0:T(8,128)S(1)}) custom-call(f32[16]{0:T(128)S(1)} %copy-done.12, f32[16]{0:T(128)S(1)} %copy-done.13, f32[16,64,128]{2,1,0:T(8,128)S(1)} %copy-done.1, f32[16,64,128]{2,1,0:T(8,128)S(1)} %copy-done.3, f32[16,64,128]{2,1,0:T(8,128)S(1)} %copy-done.5, f32[16,64,128]{2,1,0:T(8,128)S(1)} %copy-done.7, ...), custom_call_target="tpu_custom_call" | custom-call | flops 2000000 | bytes 6000000 | tf_op jit(solution)/shard_map/edge_rows/pallas_call | solution.py:551
  32.0 0.0 collective-permute-done.2.refs_2_
  32.0 0.0 collective-permute-done.3.refs_3_
  32.0 4.1 %finish.1 = (f32[16,64,128]{2,1,0:T(8,128)}, f32[16,64,128]{2,1,0:T(8,128)}, f32[16,64,128]{2,1,0:T(8,128)}, f32[16,64,128]{2,1,0:T(8,128)}) custom-call(f32[16]{0:T(128)S(1)} %copy-done.12, f32[16]{0:T(128)S(1)} %copy-done.13, f32[144,128]{1,0:T(8,128)S(1)} %collective-permute-done.2.refs_2_, f32[144,128]{1,0:T(8,128)S(1)} %collective-permute-done.3.refs_3_, ...), custom_call_target="tpu_custom_call" | custom-call | flops 2000000 | bytes 6000000 | tf_op jit(solution)/shard_map/finish/pallas_call | solution.py:567
  (17 shorter events, 0.0 us)
Async XLA Ops:
  0.6 1.0 %copy-start = (f32[16,64,128]{2,1,0:T(8,128)S(1)}, f32[16,64,128]{2,1,0:T(8,128)}, u32[]{:S(2)}) copy-start(f32[16,64,128]{2,1,0:T(8,128)} %refs_2_.3) | copy-start | bytes 1572868
  1.7 1.0 %copy-start.2 = (f32[16,64,128]{2,1,0:T(8,128)S(1)}, f32[16,64,128]{2,1,0:T(8,128)}, u32[]{:S(2)}) copy-start(f32[16,64,128]{2,1,0:T(8,128)} %refs_3_.3) | copy-start | bytes 1572868
  2.7 1.0 %copy-start.4 = (f32[16,64,128]{2,1,0:T(8,128)S(1)}, f32[16,64,128]{2,1,0:T(8,128)}, u32[]{:S(2)}) copy-start(f32[16,64,128]{2,1,0:T(8,128)} %refs_4_.3) | copy-start | bytes 1572868
  3.8 1.0 %copy-start.6 = (f32[16,64,128]{2,1,0:T(8,128)S(1)}, f32[16,64,128]{2,1,0:T(8,128)}, u32[]{:S(2)}) copy-start(f32[16,64,128]{2,1,0:T(8,128)} %refs_5_.3) | copy-start | bytes 1572868
  4.8 0.8 %copy-start.8 = (s32[64,128]{1,0:T(8,128)S(1)}, s32[64,128]{1,0:T(8,128)}, u32[]{:S(2)}) copy-start(s32[64,128]{1,0:T(8,128)} %refs_6_.3) | copy-start | bytes 98308
  5.6 0.8 %copy-start.9 = (f32[64,128]{1,0:T(8,128)S(1)}, f32[64,128]{1,0:T(8,128)}, u32[]{:S(2)}) copy-start(f32[64,128]{1,0:T(8,128)} %refs_7_.3) | copy-start | bytes 98308
  6.3 0.8 %copy-start.10 = (f32[64,128]{1,0:T(8,128)S(1)}, f32[64,128]{1,0:T(8,128)}, u32[]{:S(2)}) copy-start(f32[64,128]{1,0:T(8,128)} %refs_8_.3) | copy-start | bytes 98308
  7.1 0.8 %copy-start.11 = (f32[64,128]{1,0:T(8,128)S(1)}, f32[64,128]{1,0:T(8,128)}, u32[]{:S(2)}) copy-start(f32[64,128]{1,0:T(8,128)} %refs_9_.3) | copy-start | bytes 98308
  7.8 6.7 %copy-start.12 = (f32[16]{0:T(128)S(1)}, f32[16]{0:T(128)}, u32[]{:S(2)}) copy-start(f32[16]{0:T(128)} %refs_0_.5) | copy-start | bytes 196
  7.8 6.7 %copy-start.13 = (f32[16]{0:T(128)S(1)}, f32[16]{0:T(128)}, u32[]{:S(2)}) copy-start(f32[16]{0:T(128)} %refs_1_.5) | copy-start | bytes 196
  7.8 21.1 %copy-start.1 = (f32[16,64,128]{2,1,0:T(8,128)S(1)}, f32[16,64,128]{2,1,0:T(8,128)}, u32[]{:S(2)}) copy-start(f32[16,64,128]{2,1,0:T(8,128)} %refs_2_.3) | copy-start | bytes 1572868
  7.8 21.1 %copy-start.3 = (f32[16,64,128]{2,1,0:T(8,128)S(1)}, f32[16,64,128]{2,1,0:T(8,128)}, u32[]{:S(2)}) copy-start(f32[16,64,128]{2,1,0:T(8,128)} %refs_3_.3) | copy-start | bytes 1572868
  7.8 21.1 %copy-start.5 = (f32[16,64,128]{2,1,0:T(8,128)S(1)}, f32[16,64,128]{2,1,0:T(8,128)}, u32[]{:S(2)}) copy-start(f32[16,64,128]{2,1,0:T(8,128)} %refs_4_.3) | copy-start | bytes 1572868
  7.9 21.1 %copy-start.7 = (f32[16,64,128]{2,1,0:T(8,128)S(1)}, f32[16,64,128]{2,1,0:T(8,128)}, u32[]{:S(2)}) copy-start(f32[16,64,128]{2,1,0:T(8,128)} %refs_5_.3) | copy-start | bytes 1572868
  8.2 13.2 %collective-permute-start = (f32[208,128]{1,0:T(8,128)S(1)}, f32[208,128]{1,0:T(8,128)S(1)}, u32[]{:S(2)}, u32[]{:S(2)}) collective-permute-start(f32[208,128]{1,0:T(8,128)S(1)} %get-tuple-element.20), channel_id=1, source_target_pairs={{0,16},{1,17},{2,18},{3,19},{4,20},{5,21},{6,22},{7,23},{8,24},{9,... | collective-permute-start | bytes 319496 | tf_op jit(solution)/shard_map/ppermute | solution.py:528
  11.6 9.9 %collective-permute-start.1 = (f32[208,128]{1,0:T(8,128)S(1)}, f32[208,128]{1,0:T(8,128)S(1)}, u32[]{:S(2)}, u32[]{:S(2)}) collective-permute-start(f32[208,128]{1,0:T(8,128)S(1)} %get-tuple-element.21), channel_id=1, source_target_pairs={{16,32},{17,33},{18,34},{19,35},{20,36},{21,37},{22,38},{23,39},{2... | collective-permute-start | bytes 319496 | tf_op jit(solution)/shard_map/ppermute | solution.py:527
  22.1 9.9 %collective-permute-start.2 = (f32[144,128]{1,0:T(8,128)S(1)}, f32[144,128]{1,0:T(8,128)S(1)}, u32[]{:S(2)}, u32[]{:S(2)}) collective-permute-start(f32[144,128]{1,0:T(8,128)S(1)} %get-tuple-element.26), channel_id=1, source_target_pairs={{0,1},{1,0},{2,3},{3,2},{4,5},{5,4},{6,7},{7,6},{8,9},{9,8},{10,11... | collective-permute-start | bytes 221192 | tf_op jit(solution)/shard_map/ppermute | solution.py:550
  22.5 9.5 %collective-permute-start.3 = (f32[144,128]{1,0:T(8,128)S(1)}, f32[144,128]{1,0:T(8,128)S(1)}, u32[]{:S(2)}, u32[]{:S(2)}) collective-permute-start(f32[144,128]{1,0:T(8,128)S(1)} %get-tuple-element.27), channel_id=1, source_target_pairs={{0,15},{1,2},{2,1},{3,4},{4,3},{5,6},{6,5},{7,8},{8,7},{9,10},{10,... | collective-permute-start | bytes 221192 | tf_op jit(solution)/shard_map/ppermute | solution.py:549
where the time goes:
time: 36.6 us; the launch traced here: 36.1 us
  Pallas kernels  15 us (41%)
  starting transfers between devices  13.1 us (36%)
  local copies, waits for them, and re-layouts  7.21 us (20%)
  between operations  0.76 us (2%)
    unnamed x28, local copies, waits for them, and re-layouts  7.21 us
    pallas_call x1, Pallas kernels, on_device(): pl.pallas_call(lambda *refs: inside_kernel((0, SPLIT), *refs), out_shape=...  6.93 us
    ppermute x1, starting transfers between devices, on_device(): p2 = lax.ppermute(q2, axes, far)  6.44 us
    pallas_call x1, Pallas kernels, on_device(): pl.pallas_call(lambda *refs: finish(SPLIT, *refs), out_shape=(sds(NK, NR,...  4.1 us
    ppermute x1, starting transfers between devices, on_device(): r1 = lax.ppermute(m1, axes, near)  3.33 us
    pallas_call x1, Pallas kernels, on_device(): pl.pallas_call(lambda *refs: edge_kernel((SPLIT, NK), *refs), out_shape=(...  2.99 us
    ppermute x1, starting transfers between devices, on_device(): r2 = lax.ppermute(m2, axes, far)  2.95 us
  transfers between devices with their start and end apart: 4, of which 0 were waited for; matrix products, arithmetic and copies ran while one was open for 0% of the time, Pallas kernels for 27%

commit v1 on v0

v1 whole, which is shorter than its diff:
```python
import jax
import jax.numpy as jnp
from jax import lax
from jax.experimental import pallas as pl
from jax.experimental.pallas import tpu as pltpu
from jax.sharding import PartitionSpec as P


STEPS = 3
NF = 4
NK = 16
NR = 64
NC = 128
HALO = 3
MSG = 208
GH = 216
SR = 88
OFF = 10
NB = 8
NT = 9

F32 = jnp.float32
VM = pl.BlockSpec(memory_space=pltpu.VMEM)
HB = pl.BlockSpec(memory_space=pltpu.HBM)


def params(mib):
    return pltpu.CompilerParams(vmem_limit_bytes=mib * 2**20)


def lanes():
    return lax.broadcasted_iota(jnp.int32, (8, NC), 1)


def pick(x, index):
    return jnp.take_along_axis(x, index, axis=1, mode="promise_in_bounds")


def metric(wd, ht, cor):
    iw, ih = 1.0 / wd, 1.0 / ht
    a2, b2 = 0.2 * (iw * iw), 0.2 * (ih * ih)
    return 0.1 * iw, 0.1 * ih, 0.2 * cor, a2, b2, -2.0 * (a2 + b2)


def weights(met, wet, mix):
    a1, b1, f2, a2, b2, c2 = [jnp.where(wet, x, 0.0) for x in met]
    return (a1, b1, f2) + tuple(x for d in mix for x in (d * a2, d * b2, 1.0 + d * c2))


def advance(c, e, w, n, s, co):
    p, r = co[0] * c[2], co[1] * c[3]
    out = []
    for pair in (0, 2):
        ax, by, cc = co[3 + 3 * (pair // 2) : 6 + 3 * (pair // 2)]
        ce, cw, cn, cs = ax - p, ax + p, by - r, by + r
        for q in (pair, pair + 1):
            v = (ce * e[q] + cw * w[q]) + (cn * n[q] + cs * s[q]) + cc * c[q]
            if q == 2:
                v = v + co[2] * c[3]
            if q == 3:
                v = v - co[2] * c[2]
            out.append(v)
    return out


def pack_rows(t, s, u, v, bat, wd, ht, cor, m1, m2, fl, pn, ibuf, sems):
    lat = lax.axis_index("lat")
    last = lax.axis_size("lat") - 1
    copies = []
    for side in (0, 1):
        rows = pl.ds(side * (NR - 8), 8)
        for q, x in enumerate((t, s, u, v)):
            copies.append(
                pltpu.make_async_copy(x.at[:, rows, :], fl.at[q, side], sems.at[4 * side + q])
            )
    for q, x in enumerate((wd, ht, cor)):
        copies.append(pltpu.make_async_copy(x, pn.at[q], sems.at[8 + q]))
    copies.append(pltpu.make_async_copy(bat, ibuf, sems.at[11]))
    for c in copies:
        c.start()
    zero = jnp.zeros((8, NC), F32)
    m1[MSG - 8 : MSG, :] = zero
    m2[MSG - 8 : MSG, :] = zero
    for c in copies:
        c.wait()
    for r in (0, NR - 8):
        pn[3, r : r + 8, :] = ibuf[r : r + 8, :].astype(F32)
    base = NF * NK * HALO

    def plain(dst, side):
        r0 = 0 if side == 0 else NR - HALO
        for q in range(NF):
            for k in range(NK):
                i = (q * NK + k) * HALO
                dst[i : i + HALO, :] = fl[q, side, k, r0 % 8 : r0 % 8 + HALO, :]
        for q in range(4):
            i = base + q * HALO
            dst[i : i + HALO, :] = pn[q, r0 : r0 + HALO, :]

    def folded(dst):
        back = NC - 1 - lanes()
        for q in range(NF + 1):
            for k in range(NK if q < NF else 4):
                x = fl[q, 1, k, :, :] if q < NF else pn[k, NR - 8 : NR, :]
                x = pick(x, back)
                x = -x if q in (2, 3) else x
                i = (q * NK + k) * HALO
                for m in range(HALO):
                    dst[i + m : i + m + 1, :] = x[7 - m : 8 - m, :]

    odd = lax.rem(lat, 2) == 1

    @pl.when(jnp.logical_not(odd))
    def _():
        plain(m2, 0)
        plain(m1, 1)

    @pl.when(odd)
    def _():
        plain(m1, 0)

    @pl.when(jnp.logical_and(odd, lat != last))
    def _():
        plain(m2, 1)

    @pl.when(lat == last)
    def _():
        folded(m2)


PAIR = 2


def interior(levels, fl, bat, mix, met, a, b, cf, out):
    def level(i, carry):
        ks = [levels[0] + i * PAIR + g for g in range(PAIR)]
        for g, k in enumerate(ks):
            ds = [mix[m, pl.ds(k, 1), :] for m in (0, 1)]
            for j in range(8):
                rows = slice(8 * j, 8 * j + 8)
                wet = k < bat[rows, :]
                for m, x in enumerate(weights([met[m, rows, :] for m in range(6)], wet, ds)):
                    cf[g, m, rows, :] = x
                for q in range(NF):
                    a[g, q, 8 + 8 * j : 16 + 8 * j, :] = jnp.where(wet, fl[q][k, rows, :], 0.0)
        src, dst = a, b
        for step in range(STEPS):
            for j in range(8):
                for g, k in enumerate(ks):
                    r = 8 + 8 * j
                    rows = slice(8 * j, 8 * j + 8)
                    c = [src[g, q, r : r + 8, :] for q in range(NF)]
                    n = [src[g, q, r + 1 : r + 9, :] for q in range(NF)]
                    s = [src[g, q, r - 1 : r + 7, :] for q in range(NF)]
                    e = [pltpu.roll(x, NC - 1, 1) for x in c]
                    w = [pltpu.roll(x, 1, 1) for x in c]
                    new = advance(c, e, w, n, s, [cf[g, m, rows, :] for m in range(9)])
                    for q in range(NF):
                        if step == STEPS - 1:
                            out[q, k, rows, :] = new[q]
                        else:
                            dst[g, q, r : r + 8, :] = new[q]
            src, dst = dst, src
        return carry

    lax.fori_loop(0, (levels[1] - levels[0]) // PAIR, level, 0)


def start_interior(planes, met, a, b):
    zero = jnp.zeros((8, NC), F32)
    for g in range(PAIR):
        for q in range(NF):
            for x in (a, b):
                x[g, q, 0:8, :] = zero
                x[g, q, NR + 8 : NR + 16, :] = zero
    for j in range(8):
        rows = slice(8 * j, 8 * j + 8)
        for i, x in enumerate(metric(*[x[rows, :] for x in planes])):
            met[i, rows, :] = x


def strip_index():
    lane = lanes()
    level, block = lane // NB, lane % NB
    west = jnp.where(block >= HALO, block - HALO, NC - 6)
    east = jnp.where(block < 5, block + NC - 5, 5)
    return level, west, east


def inside_kernel(levels, mix, t, s, u, v, wd, ht, cor, bat, out, gw, ge, pw, pe, met, a, b, cf):
    fl, pn = (t, s, u, v), (wd, ht, cor, bat)
    level, west, east = strip_index()
    for j in range(8):
        rows = slice(8 * j, 8 * j + 8)
        for q in range(NF):
            xw = xe = jnp.zeros((8, NC), F32)
            for k in range(NK):
                x = fl[q][k, rows, :]
                here = level == k
                xw = jnp.where(here, pick(x, west), xw)
                xe = jnp.where(here, pick(x, east), xe)
            gw[q, rows, :] = xw
            ge[q, rows, :] = xe
            x = pn[q][rows, :].astype(F32)
            pw[q, rows, :] = pick(x, west)
            pe[q, rows, :] = pick(x, east)
    start_interior(pn[:3], met, a, b)
    interior(levels, fl, bat, mix, met, a, b, cf, out)


def pack_columns(r1, r2, gw, ge, pw, pe, q1, q2, gh, sw, se, spw, spe):
    odd = lax.rem(lax.axis_index("lat"), 2) == 1
    even_lon = lax.rem(lax.axis_index("lon"), 2) == 0
    for i in range(MSG // 8):
        rows = slice(8 * i, 8 * i + 8)
        x1, x2 = r1[rows, :], r2[rows, :]
        gh[0, rows, :] = jnp.where(odd, x1, x2)
        gh[1, rows, :] = jnp.where(odd, x2, x1)
    zero = jnp.zeros((8, NC), F32)
    gh[0, MSG:GH, :] = zero
    gh[1, MSG:GH, :] = zero
    level, west, east = strip_index()
    for own, strip in ((gw, sw), (ge, se), (pw, spw), (pe, spe)):
        for q in range(4):
            strip[q, 0:8, :] = zero
            strip[q, 72:80, :] = zero
            strip[q, 80:88, :] = zero
            for j in range(8):
                strip[q, OFF + 8 * j : OFF + 8 * j + 8, :] = own[q, 8 * j : 8 * j + 8, :]
    for side, at in ((0, OFF - HALO), (1, OFF + NR)):
        for q in range(NF):
            xw = xe = zero
            for k in range(NK):
                i = (q * NK + k) * HALO
                x = gh[side, i : i + 8, :]
                here = level == k
                xw = jnp.where(here, pick(x, west), xw)
                xe = jnp.where(here, pick(x, east), xe)
            sw[q, at : at + HALO, :] = xw[:HALO, :]
            se[q, at : at + HALO, :] = xe[:HALO, :]
            i = NF * NK * HALO + q * HALO
            x = gh[side, i : i + 8, :]
            spw[q, at : at + HALO, :] = pick(x, west)[:HALO, :]
            spe[q, at : at + HALO, :] = pick(x, east)[:HALO, :]
    lane = lanes()
    level, block = lane // NB, lane % NB
    first, second = block < HALO, block < 2 * HALO
    nth = jnp.where(second, 0, level * 2 + block - 6)
    plane, column = nth // HALO, lax.rem(nth, HALO)

    def emit(dst_e, dst_w):
        for dst, strip, planes, start in ((dst_e, se, spe, 2), (dst_w, sw, spw, 3)):
            for i in range(NT):
                rows = slice(OFF - HALO + 8 * i, OFF - HALO + 8 * i + 8)
                for pair in (0, 1):
                    x = pltpu.roll(strip[2 * pair, rows, :], NC - start, 1)
                    y = strip[2 * pair + 1, rows, :]
                    if start != HALO:
                        y = pltpu.roll(y, HALO - start, 1)
                    z = jnp.where(first, x, y)
                    if pair == 0:
                        for m in range(4):
                            take = jnp.logical_and(plane == m, jnp.logical_not(second))
                            z = jnp.where(take, pick(planes[m, rows, :], start + column), z)
                    dst[pair * 8 * NT + 8 * i : pair * 8 * NT + 8 * i + 8, :] = z

    @pl.when(even_lon)
    def _():
        emit(q1, q2)

    @pl.when(jnp.logical_not(even_lon))
    def _():
        emit(q2, q1)


def edge_rows(mix, fl, pn, gh, out, win, pwin):
    base = NF * NK * HALO
    own = ((0, 10), (NR - 8, 6))
    ghost = (7, 14)
    met, wets, gwets = [], [], []
    for side in (0, 1):
        r0, at = own[side]
        g = ghost[side]
        for i in range(4):
            pwin[side, i, at : at + 8, :] = pn[i][r0 : r0 + 8, :].astype(F32)
            pwin[side, i, g : g + HALO, :] = gh[side, base + i * HALO : base + (i + 1) * HALO, :]
        met.append(metric(*[pwin[side, i, 8:16, :] for i in range(3)]))
        wets.append(pwin[side, 3, 8:16, :])
        gwets.append(gh[side, base + 3 * HALO : base + 4 * HALO, :])
    group = 2

    def body(i, carry):
        work, state = [], []
        for g in range(group):
            k = i * group + g
            kf = k.astype(F32)
            ds = [mix[m, pl.ds(k, 1), :] for m in (0, 1)]
            for side in (0, 1):
                r0, at = own[side]
                gr = ghost[side]
                wet_own = k < pn[3][r0 : r0 + 8, :]
                wet_ghost = kf < gwets[side]
                for q in range(NF):
                    win[g, side, q, at : at + 8, :] = jnp.where(
                        wet_own, fl[q][k, r0 : r0 + 8, :], 0.0
                    )
                    x = gh[side, pl.ds((q * NK + k) * HALO, HALO), :]
                    win[g, side, q, gr : gr + HALO, :] = jnp.where(wet_ghost, x, 0.0)
                work.append((g, side, k, weights(met[side], kf < wets[side], ds)))
        for g, side, k, co in work:
            c = [win[g, side, q, 8:16, :] for q in range(NF)]
            n = [win[g, side, q, 9:17, :] for q in range(NF)]
            s = [win[g, side, q, 7:15, :] for q in range(NF)]
            state.append((c, n, s))
        for step in range(STEPS):
            nxt = []
            for (g, side, k, co), (c, n, s) in zip(work, state):
                e = [pltpu.roll(x, NC - 1, 1) for x in c]
                w = [pltpu.roll(x, 1, 1) for x in c]
                c = advance(c, e, w, n, s, co)
                n = s = None
                if step < STEPS - 1:
                    n = [pltpu.roll(x, 7, 0) for x in c]
                    s = [pltpu.roll(x, 1, 0) for x in c]
                nxt.append((c, n, s))
            state = nxt
        for (g, side, k, co), (c, _, _) in zip(work, state):
            for q in range(NF):
                out[side, q, k, :, :] = pltpu.roll(c[q], 6 if side == 0 else 2, 0)
        return carry

    lax.fori_loop(0, NK // group, body, 0)


def edge_kernel(
    levels, mix, t, s, u, v, wd, ht, cor, bat, gh, out, more, win, pwin, met, a, b, cf
):
    fl, pn = (t, s, u, v), (wd, ht, cor, bat)
    edge_rows(mix, fl, pn, gh, out, win, pwin)
    if levels[0] < levels[1]:
        start_interior(pn[:3], met, a, b)
        interior(levels, fl, bat, mix, met, a, b, cf, more)


def finish(
    split, mix, q1, q2, sw, se, spw, spe, rows_new, inner, inner2,
    ot, os, ou, ov, aw, ae, bw, be, cw, ce, zed, res, sems,
):
    even = lax.rem(lax.axis_index("lon"), 2) == 0
    lane = lanes()
    level, block = lane // NB, lane % NB
    ds = [jnp.zeros((8, NC), F32)] * 2
    for k in range(NK):
        here = level == k
        ds = [jnp.where(here, mix[m, k : k + 1, :], ds[m]) for m in (0, 1)]
    level_f = level.astype(F32)
    zero = jnp.zeros((8, NC), F32)
    sides = (
        (0, aw, bw, cw, sw, spw, block < HALO, block, (0, 125)),
        (1, ae, be, ce, se, spe, block >= 5, block - 5, (5, 2)),
    )
    for side, a, b, co, strip, planes, from_ghost, column, shifts in sides:
        column = jnp.clip(column, 0, HALO - 1)
        which = []
        for m in range(4):
            nth = m * HALO + column
            which.append((nth // 2) * NB + 6 + lax.rem(nth, 2))
        for x in (a, b):
            for q in range(NF):
                x[q, 0:8, :] = zero
                x[q, 80:88, :] = zero
        for i in range(NT):
            rows = slice(OFF - HALO + 8 * i, OFF - HALO + 8 * i + 8)
            g = []
            for pair in (0, 1):
                at = slice(pair * 8 * NT + 8 * i, pair * 8 * NT + 8 * i + 8)
                x1, x2 = q1[at, :], q2[at, :]
                g.append(
                    jnp.where(even, x2, x1) if side == 0 else jnp.where(even, x1, x2)
                )
            pls = [
                jnp.where(from_ghost, pick(g[0], which[m]), planes[m, rows, :]) for m in range(4)
            ]
            wet = level_f < pls[3]
            for m, x in enumerate(weights(metric(*pls[:3]), wet, ds)):
                co[m, rows, :] = x
            for q in range(NF):
                sh = shifts[q % 2]
                x = g[q // 2] if sh == 0 else pltpu.roll(g[q // 2], sh, 1)
                x = jnp.where(from_ghost, x, strip[q, rows, :])
                a[q, rows, :] = jnp.where(wet, x, 0.0)
    extra_w, extra_e = block == 7, block == 0
    for step in range(STEPS):
        for i in range(NT):
            r = 8 + 8 * i
            for side, a, b, co, strip, planes, from_ghost, column, shifts in sides:
                src, dst = (a, b) if step % 2 == 0 else (b, a)
                c = [src[q, r : r + 8, :] for q in range(NF)]
                n = [src[q, r + 1 : r + 9, :] for q in range(NF)]
                s = [src[q, r - 1 : r + 7, :] for q in range(NF)]
                e = [pltpu.roll(x, NC - 1, 1) for x in c]
                w = [pltpu.roll(x, 1, 1) for x in c]
                if step == 0:
                    if side == 0:
                        wet = jnp.logical_and(extra_w, level_f < spe[3, r : r + 8, :])
                        e = [
                            jnp.where(wet, se[q, r : r + 8, :], jnp.where(extra_w, 0.0, e[q]))
                            for q in range(NF)
                        ]
                    else:
                        wet = jnp.logical_and(extra_e, level_f < spw[3, r : r + 8, :])
                        w = [
                            jnp.where(wet, sw[q, r : r + 8, :], jnp.where(extra_e, 0.0, w[q]))
                            for q in range(NF)
                        ]
                new = advance(c, e, w, n, s, [co[m, r : r + 8, :] for m in range(9)])
                for q in range(NF):
                    dst[q, r : r + 8, :] = new[q]
    fin_w, fin_e = (bw, be) if STEPS % 2 else (aw, ae)
    for q in range(NF):
        for j in range(8):
            rows = slice(OFF + 8 * j, OFF + 8 * j + 8)
            zed[q, 8 * j : 8 * j + 8, :] = jnp.where(
                block >= HALO, fin_w[q, rows, :], pltpu.roll(fin_e[q, rows, :], NC - 2, 1)
            )
    edge = jnp.logical_or(lane < HALO, lane >= NC - HALO)
    row = lax.broadcasted_iota(jnp.int32, (8, NC), 0)
    top, bottom = row < HALO, row >= 8 - HALO
    outs = (ot, os, ou, ov)
    group = 4

    def copy(q, g):
        return pltpu.make_async_copy(
            res.at[q, pl.ds(g * group, group)], outs[q].at[pl.ds(g * group, group)], sems.at[q, g]
        )

    for g in range(NK // group):
        for q in range(NF):
            for k in range(g * group, (g + 1) * group):
                src, at = (inner, k) if k < split else (inner2, k)
                for j in range(8):
                    rows = slice(8 * j, 8 * j + 8)
                    x = src[q, at, rows, :]
                    if j == 0:
                        x = jnp.where(top, rows_new[0, q, k, :, :], x)
                    if j == 7:
                        x = jnp.where(bottom, rows_new[1, q, k, :, :], x)
                    y = pltpu.roll(zed[q, rows, :], (NC - HALO - NB * k) % NC, 1)
                    res[q, k, rows, :] = jnp.where(edge, y, x)
            copy(q, g).start()
    for g in range(NK // group):
        for q in range(NF):
            copy(q, g).wait()


def row_pairs(nl, no):
    near, far = [], []
    for j in range(nl):
        for i in range(no):
            near.append((j * no + i, (j ^ 1) * no + i))
            if j == nl - 1:
                far.append((j * no + i, j * no + no - 1 - i))
            elif j % 2:
                far.append((j * no + i, (j + 1) * no + i))
            elif j > 0:
                far.append((j * no + i, (j - 1) * no + i))
    return near, far


def column_pairs(nl, no):
    near, far = [], []
    for j in range(nl):
        for i in range(no):
            near.append((j * no + i, j * no + (i ^ 1)))
            far.append((j * no + i, j * no + ((i + 1) % no if i % 2 else (i - 1) % no)))
    return near, far


SPLIT = 12


def on_device(t, s, u, v, bat, wd, ht, cor, mt, ms):
    nl, no = lax.axis_size("lat"), lax.axis_size("lon")
    axes = ("lat", "lon")
    sds = lambda *shape: jax.ShapeDtypeStruct(shape, F32)
    vm = lambda *shape: pltpu.VMEM(shape, F32)
    cost = lambda us: pl.CostEstimate(
        flops=int(us * 1e6), bytes_accessed=int(us * 3e6), transcendentals=0
    )
    mix = jnp.broadcast_to(jnp.stack([mt, ms])[:, :, None], (2, NK, NC))
    m1, m2 = pl.pallas_call(
        pack_rows,
        out_shape=(sds(MSG, NC), sds(MSG, NC)),
        in_specs=[HB] * 8,
        out_specs=(VM,) * 2,
        scratch_shapes=[
            vm(NF, 2, NK, 8, NC),
            vm(4, NR, NC),
            pltpu.VMEM((NR, NC), jnp.int32),
            pltpu.SemaphoreType.DMA((12,)),
        ],
        compiler_params=params(58),
        cost_estimate=cost(1),
        name="pack_rows",
    )(t, s, u, v, bat, wd, ht, cor)
    near, far = row_pairs(nl, no)
    r2 = lax.ppermute(m2, axes, far)
    r1 = lax.ppermute(m1, axes, near)
    work = [vm(6, NR, NC), vm(PAIR, NF, 80, NC), vm(PAIR, NF, 80, NC), vm(PAIR, 9, NR, NC)]
    inner, gw, ge, pw, pe = pl.pallas_call(
        lambda *refs: inside_kernel((0, SPLIT), *refs),
        out_shape=(sds(NF, SPLIT, NR, NC),) + (sds(4, NR, NC),) * 4,
        in_specs=[VM] * 9,
        out_specs=(VM,) * 5,
        scratch_shapes=work,
        compiler_params=params(6),
        cost_estimate=cost(4),
        name="inside",
    )(mix, t, s, u, v, wd, ht, cor, bat)
    q1, q2, gh, sw, se, spw, spe = pl.pallas_call(
        pack_columns,
        out_shape=(sds(16 * NT, NC),) * 2 + (sds(2, GH, NC),) + (sds(4, SR, NC),) * 4,
        in_specs=[VM] * 6,
        out_specs=(VM,) * 7,
        compiler_params=params(6),
        cost_estimate=cost(1),
        name="pack_columns",
    )(r1, r2, gw, ge, pw, pe)
    near, far = column_pairs(nl, no)
    p2 = lax.ppermute(q2, axes, far)
    p1 = lax.ppermute(q1, axes, near)
    rows_new, inner2 = pl.pallas_call(
        lambda *refs: edge_kernel((SPLIT, NK), *refs),
        out_shape=(sds(2, NF, NK, 8, NC), sds(NF, NK, NR, NC)),
        in_specs=[VM] * 10,
        out_specs=(VM,) * 2,
        scratch_shapes=[vm(2, 2, NF, 24, NC), vm(2, 4, 24, NC)] + work,
        compiler_params=params(6),
        cost_estimate=cost(2),
        name="edge_rows",
    )(mix, t, s, u, v, wd, ht, cor, bat, gh)
    return pl.pallas_call(
        lambda *refs: finish(SPLIT, *refs),
        out_shape=(sds(NK, NR, NC),) * 4,
        in_specs=[VM] * 10,
        out_specs=(HB,) * 4,
        scratch_shapes=[vm(NF, SR, NC)] * 4
        + [vm(9, SR, NC)] * 2
        + [vm(NF, NR, NC), vm(NF, NK, NR, NC), pltpu.SemaphoreType.DMA((NF, 4))],
        compiler_params=params(8),
        cost_estimate=cost(2),
        name="finish",
    )(mix, p1, p2, sw, se, spw, spe, rows_new, inner, inner2)


def solution(mesh):
    block = P(None, "lat", "lon")
    plane = P("lat", "lon")
    return jax.shard_map(
        on_device,
        mesh=mesh,
        in_specs=(block,) * 4 + (plane,) * 4 + (P(), P()),
        out_specs=(block,) * 4,
        check_vma=False,
    )
```

time: 36.6 us -> 26.7 us (0.73); the launches traced: 36.1 us -> 26.5 us
  local copies, waits for them, and re-layouts: 7.21 us -> 0.11 us
  Pallas kernels: 15 us -> 12.6 us
  starting transfers between devices: 13.1 us -> 12.4 us
  waiting for transfers between devices: 0.01 us -> 0.59 us
    unnamed x28 -> x20, local copies, waits for them, and re-layouts: 7.21 us -> 0.04 us
    pallas_call x1, Pallas kernels: 6.93 us -> 4.13 us  [on_device(): pl.pallas_call(lambda *refs: inside_kernel((0, SPLIT), *refs), out_shape=...]
    pallas_call x1, Pallas kernels: 4.1 us -> 2.38 us  [on_device(): pl.pallas_call(lambda *refs: finish(SPLIT, *refs), out_shape=(sds(NK, NR,...]
    pallas_call x1, Pallas kernels: 0.36 us -> 2.05 us  [on_device(): pl.pallas_call(pack_rows, out_shape=(sds(MSG, NC), sds(MSG, NC)), in_spec...]
    ppermute x1, starting transfers between devices: 6.44 us -> 5.82 us  [on_device(): p2 = lax.ppermute(q2, axes, far)]
    ppermute x1, waiting for transfers between devices: 0.01 us -> 0.59 us  [on_device(): r2 = lax.ppermute(m2, axes, far)]
    pallas_call x1, Pallas kernels: 2.99 us -> 3.42 us  [on_device(): pl.pallas_call(lambda *refs: edge_kernel((SPLIT, NK), *refs), out_shape=(...]
  transfers between devices with their start and end apart: 4 -> 4, of which waited for: 0 -> 1; matrix products, arithmetic and copies ran while one was open for 0% -> 0% of each run, Pallas kernels for 27% -> 28%
where the time goes in v1:
time: 26.7 us; the launch traced here: 26.5 us
  Pallas kernels  12.6 us (47%)
  starting transfers between devices  12.4 us (46%)
  between operations  0.85 us (3%)
  waiting for transfers between devices  0.59 us (2%)
    ppermute x1, starting transfers between devices, on_device(): p2 = lax.ppermute(q2, axes, far)  5.82 us
    pallas_call x1, Pallas kernels, on_device(): pl.pallas_call(lambda *refs: inside_kernel((0, SPLIT), *refs), out_shape=...  4.13 us
    pallas_call x1, Pallas kernels, on_device(): pl.pallas_call(lambda *refs: edge_kernel((SPLIT, NK), *refs), out_shape=(...  3.42 us
    ppermute x1, starting transfers between devices, on_device(): r1 = lax.ppermute(m1, axes, near)  3.34 us
    ppermute x1, starting transfers between devices, on_device(): r2 = lax.ppermute(m2, axes, far)  2.81 us
    pallas_call x1, Pallas kernels, on_device(): pl.pallas_call(lambda *refs: finish(SPLIT, *refs), out_shape=(sds(NK, NR,...  2.38 us
    pallas_call x1, Pallas kernels, on_device(): pl.pallas_call(pack_rows, out_shape=(sds(MSG, NC), sds(MSG, NC)), in_spec...  2.05 us
    ppermute x1, waiting for transfers between devices, on_device(): r2 = lax.ppermute(m2, axes, far)  0.59 us
  transfers between devices with their start and end apart: 4, of which 1 were waited for; matrix products, arithmetic and copies ran while one was open for 0% of the time, Pallas kernels for 28%

profile of v1, /device:TPU:1, one launch (start us, length us, event | category | flops | bytes accessed | tf_op | source)
XLA Modules:
  0.0 26.5 jit_solution(3707187921720962769)
XLA Ops:
  0.6 0.0 copy-start.7
  0.6 0.0 copy-start.6
  0.7 0.0 copy-start.5
  0.7 0.0 copy-start.4
  0.7 0.0 copy-start.3
  0.7 0.0 copy-start.2
  0.7 0.0 copy-start.1
  0.7 0.0 copy-start
  0.7 0.0 copy-start.8
  0.7 0.0 copy-start.9
  0.7 2.1 %pack_rows.1 = (f32[208,128]{1,0:T(8,128)}, f32[208,128]{1,0:T(8,128)}) custom-call(f32[16,64,128]{2,1,0:T(8,128)} %refs_1_.3, f32[16,64,128]{2,1,0:T(8,128)} %refs_2_.3, f32[16,64,128]{2,1,0:T(8,128)} %refs_3_.3, f32[16,64,128]{2,1,0:T(8,128)} %refs_4_.3, s32[64,128]{1,0:T(8,128)} %refs_8_.3, f32[64,128]{1,0:T(8,128)} %refs_5_.3, f32[64,128]{1,0:T(8,128)} %refs_6_.3, ...), custom_call_target="tpu_custom_call" | custom-call | flops 1000000 | bytes 3000000 | tf_op jit(solution)/shard_map/pack_rows/pallas_call | solution.py:491
  2.8 3.3 %collective-permute-start = (f32[208,128]{1,0:T(8,128)}, f32[208,128]{1,0:T(8,128)S(1)}, u32[]{:S(2)}, u32[]{:S(2)}) collective-permute-start(f32[208,128]{1,0:T(8,128)} %get-tuple-element.20), channel_id=1, source_target_pairs={{0,16},{1,17},{2,18},{3,19},{4,20},{5,21},{6,22},{7,23},{8,24},{9,... | collective-permute-start | bytes 319496 | tf_op jit(solution)/shard_map/ppermute | solution.py:508
  6.1 2.8 %collective-permute-start.1 = (f32[208,128]{1,0:T(8,128)}, f32[208,128]{1,0:T(8,128)S(1)}, u32[]{:S(2)}, u32[]{:S(2)}) collective-permute-start(f32[208,128]{1,0:T(8,128)} %get-tuple-element.21), channel_id=1, source_target_pairs={{16,32},{17,33},{18,34},{19,35},{20,36},{21,37},{22,38},{23,39},{2... | collective-permute-start | bytes 319496 | tf_op jit(solution)/shard_map/ppermute | solution.py:507
  9.0 0.1 broadcast_in_dim.2.refs_0_
  9.1 4.1 %inside.1 = (f32[4,12,64,128]{3,2,1,0:T(8,128)S(1)}, f32[4,64,128]{2,1,0:T(8,128)S(1)}, f32[4,64,128]{2,1,0:T(8,128)S(1)}, f32[4,64,128]{2,1,0:T(8,128)S(1)}, f32[4,64,128]{2,1,0:T(8,128)S(1)}) custom-call(f32[2,16,128]{2,1,0:T(8,128)S(1)} %broadcast_in_dim.2.refs_0_, f32[16,64,128]{2,1,0:T(8,128)S(1)} %copy-done, f32[16,64,128]{2,1,0:T(8,128)S(1)} %copy-done.1, ...), custom_call_target="tpu_custom_call" | custom-call | flops 4000000 | bytes 12000000 | tf_op jit(solution)/shard_map/inside/pallas_call | solution.py:510
  13.3 0.0 collective-permute-done.r1
  13.3 0.6 %collective-permute-done.1.r2 = f32[208,128]{1,0:T(8,128)S(1)} collective-permute-done((f32[208,128]{1,0:T(8,128)}, f32[208,128]{1,0:T(8,128)S(1)}, u32[]{:S(2)}, u32[]{:S(2)}) %collective-permute-start.1) | collective-permute-done | bytes 106528 | tf_op jit(solution)/shard_map/ppermute | solution.py:507
  13.9 0.6 %pack_columns.1 = (f32[144,128]{1,0:T(8,128)S(1)}, f32[144,128]{1,0:T(8,128)S(1)}, f32[2,216,128]{2,1,0:T(8,128)S(1)}, f32[4,88,128]{2,1,0:T(8,128)S(1)}, f32[4,...) custom-call(f32[208,128]{1,0:T(8,128)S(1)} %collective-permute-done.r1, ...), custom_call_target="tpu_custom_call" | custom-call | flops 1000000 | bytes 3000000 | tf_op jit(solution)/shard_map/pack_columns/pallas_call | solution.py:520
  14.4 0.5 %collective-permute-start.2 = (f32[144,128]{1,0:T(8,128)S(1)}, f32[144,128]{1,0:T(8,128)S(1)}, u32[]{:S(2)}, u32[]{:S(2)}) collective-permute-start(f32[144,128]{1,0:T(8,128)S(1)} %get-tuple-element.26), channel_id=1, source_target_pairs={{0,1},{1,0},{2,3},{3,2},{4,5},{5,4},{6,7},{7,6},{8,9},{9,8},{10,11... | collective-permute-start | bytes 221192 | tf_op jit(solution)/shard_map/ppermute | solution.py:531
  14.9 5.8 %collective-permute-start.3 = (f32[144,128]{1,0:T(8,128)S(1)}, f32[144,128]{1,0:T(8,128)S(1)}, u32[]{:S(2)}, u32[]{:S(2)}) collective-permute-start(f32[144,128]{1,0:T(8,128)S(1)} %get-tuple-element.27), channel_id=1, source_target_pairs={{0,15},{1,2},{2,1},{3,4},{4,3},{5,6},{6,5},{7,8},{8,7},{9,10},{10,... | collective-permute-start | bytes 221192 | tf_op jit(solution)/shard_map/ppermute | solution.py:530
  20.7 3.4 %edge_rows.1 = (f32[2,4,16,8,128]{4,3,2,1,0:T(8,128)S(1)}, f32[4,16,64,128]{3,2,1,0:T(8,128)S(1)}) custom-call(f32[2,16,128]{2,1,0:T(8,128)S(1)} %broadcast_in_dim.2.refs_0_, f32[16,64,128]{2,1,0:T(8,128)S(1)} %copy-done, f32[16,64,128]{2,1,0:T(8,128)S(1)} %copy-done.1, f32[16,64,128]{2,1,0:T(8,128)S(1)} %copy-done.2, f32[16,64,128]{2,1,0:T(8,128)S(1)} %copy-done.3, ...), custom_call_target="tpu_custom_call" | custom-call | flops 2000000 | bytes 6000000 | tf_op jit(solution)/shard_map/edge_rows/pallas_call | solution.py:532
  24.1 0.0 collective-permute-done.2.refs_1_
  24.2 0.0 collective-permute-done.3.refs_2_
  24.2 2.4 %finish.1 = (f32[16,64,128]{2,1,0:T(8,128)}, f32[16,64,128]{2,1,0:T(8,128)}, f32[16,64,128]{2,1,0:T(8,128)}, f32[16,64,128]{2,1,0:T(8,128)}) custom-call(f32[2,16,128]{2,1,0:T(8,128)S(1)} %broadcast_in_dim.2.refs_0_, f32[144,128]{1,0:T(8,128)S(1)} %collective-permute-done.2.refs_1_, f32[144,128]{1,0:T(8,128)S(1)} %collective-permute-done.3.refs_2_, ...), custom_call_target="tpu_custom_call" | custom-call | flops 2000000 | bytes 6000000 | tf_op jit(solution)/shard_map/finish/pallas_call | solution.py:542
  (11 shorter events, 0.0 us)
Async XLA Ops:
  0.6 8.4 %copy-start.7 = (f32[64,128]{1,0:T(8,128)S(1)}, f32[64,128]{1,0:T(8,128)}, u32[]{:S(2)}) copy-start(f32[64,128]{1,0:T(8,128)} %refs_7_.3) | copy-start | bytes 98308
  0.6 8.4 %copy-start.6 = (f32[64,128]{1,0:T(8,128)S(1)}, f32[64,128]{1,0:T(8,128)}, u32[]{:S(2)}) copy-start(f32[64,128]{1,0:T(8,128)} %refs_6_.3) | copy-start | bytes 98308
  0.7 8.4 %copy-start.5 = (f32[64,128]{1,0:T(8,128)S(1)}, f32[64,128]{1,0:T(8,128)}, u32[]{:S(2)}) copy-start(f32[64,128]{1,0:T(8,128)} %refs_5_.3) | copy-start | bytes 98308
  0.7 8.4 %copy-start.4 = (s32[64,128]{1,0:T(8,128)S(1)}, s32[64,128]{1,0:T(8,128)}, u32[]{:S(2)}) copy-start(s32[64,128]{1,0:T(8,128)} %refs_8_.3) | copy-start | bytes 98308
  0.7 8.4 %copy-start.3 = (f32[16,64,128]{2,1,0:T(8,128)S(1)}, f32[16,64,128]{2,1,0:T(8,128)}, u32[]{:S(2)}) copy-start(f32[16,64,128]{2,1,0:T(8,128)} %refs_4_.3) | copy-start | bytes 1572868
  0.7 8.4 %copy-start.2 = (f32[16,64,128]{2,1,0:T(8,128)S(1)}, f32[16,64,128]{2,1,0:T(8,128)}, u32[]{:S(2)}) copy-start(f32[16,64,128]{2,1,0:T(8,128)} %refs_3_.3) | copy-start | bytes 1572868
  0.7 8.4 %copy-start.1 = (f32[16,64,128]{2,1,0:T(8,128)S(1)}, f32[16,64,128]{2,1,0:T(8,128)}, u32[]{:S(2)}) copy-start(f32[16,64,128]{2,1,0:T(8,128)} %refs_2_.3) | copy-start | bytes 1572868
  0.7 8.4 %copy-start = (f32[16,64,128]{2,1,0:T(8,128)S(1)}, f32[16,64,128]{2,1,0:T(8,128)}, u32[]{:S(2)}) copy-start(f32[16,64,128]{2,1,0:T(8,128)} %refs_1_.3) | copy-start | bytes 1572868
  0.7 8.2 %copy-start.8 = (f32[16]{0:T(128)S(1)}, f32[16]{0:T(128)}, u32[]{:S(2)}) copy-start(f32[16]{0:T(128)} %param.19) | copy-start | bytes 196
  0.7 8.2 %copy-start.9 = (f32[16]{0:T(128)S(1)}, f32[16]{0:T(128)}, u32[]{:S(2)}) copy-start(f32[16]{0:T(128)} %param.18) | copy-start | bytes 196
  2.8 10.5 %collective-permute-start = (f32[208,128]{1,0:T(8,128)}, f32[208,128]{1,0:T(8,128)S(1)}, u32[]{:S(2)}, u32[]{:S(2)}) collective-permute-start(f32[208,128]{1,0:T(8,128)} %get-tuple-element.20), channel_id=1, source_target_pairs={{0,16},{1,17},{2,18},{3,19},{4,20},{5,21},{6,22},{7,23},{8,24},{9,... | collective-permute-start | bytes 319496 | tf_op jit(solution)/shard_map/ppermute | solution.py:508
  6.1 7.7 %collective-permute-start.1 = (f32[208,128]{1,0:T(8,128)}, f32[208,128]{1,0:T(8,128)S(1)}, u32[]{:S(2)}, u32[]{:S(2)}) collective-permute-start(f32[208,128]{1,0:T(8,128)} %get-tuple-element.21), channel_id=1, source_target_pairs={{16,32},{17,33},{18,34},{19,35},{20,36},{21,37},{22,38},{23,39},{2... | collective-permute-start | bytes 319496 | tf_op jit(solution)/shard_map/ppermute | solution.py:507
  14.4 9.7 %collective-permute-start.2 = (f32[144,128]{1,0:T(8,128)S(1)}, f32[144,128]{1,0:T(8,128)S(1)}, u32[]{:S(2)}, u32[]{:S(2)}) collective-permute-start(f32[144,128]{1,0:T(8,128)S(1)} %get-tuple-element.26), channel_id=1, source_target_pairs={{0,1},{1,0},{2,3},{3,2},{4,5},{5,4},{6,7},{7,6},{8,9},{9,8},{10,11... | collective-permute-start | bytes 221192 | tf_op jit(solution)/shard_map/ppermute | solution.py:531
  14.9 9.3 %collective-permute-start.3 = (f32[144,128]{1,0:T(8,128)S(1)}, f32[144,128]{1,0:T(8,128)S(1)}, u32[]{:S(2)}, u32[]{:S(2)}) collective-permute-start(f32[144,128]{1,0:T(8,128)S(1)} %get-tuple-element.27), channel_id=1, source_target_pairs={{0,15},{1,2},{2,1},{3,4},{4,3},{5,6},{6,5},{7,8},{8,7},{9,10},{10,... | collective-permute-start | bytes 221192 | tf_op jit(solution)/shard_map/ppermute | solution.py:530

commit v2 on v1

--- a/solution.py
+++ b/solution.py
@@ -287,7 +287,7 @@
         met.append(metric(*[pwin[side, i, 8:16, :] for i in range(3)]))
         wets.append(pwin[side, 3, 8:16, :])
         gwets.append(gh[side, base + 3 * HALO : base + 4 * HALO, :])
-    group = 2
+    group = 4
 
     def body(i, carry):
         work, state = [], []
@@ -488,6 +488,7 @@
         flops=int(us * 1e6), bytes_accessed=int(us * 3e6), transcendentals=0
     )
     mix = jnp.broadcast_to(jnp.stack([mt, ms])[:, :, None], (2, NK, NC))
+    hbm = [pltpu.with_memory_space_constraint(x, pltpu.HBM) for x in (t, s, u, v, bat, wd, ht, cor)]
     m1, m2 = pl.pallas_call(
         pack_rows,
         out_shape=(sds(MSG, NC), sds(MSG, NC)),
@@ -499,10 +500,10 @@
             pltpu.VMEM((NR, NC), jnp.int32),
             pltpu.SemaphoreType.DMA((12,)),
         ],
-        compiler_params=params(58),
+        compiler_params=params(6),
         cost_estimate=cost(1),
         name="pack_rows",
-    )(t, s, u, v, bat, wd, ht, cor)
+    )(*hbm)
     near, far = row_pairs(nl, no)
     r2 = lax.ppermute(m2, axes, far)
     r1 = lax.ppermute(m1, axes, near)
@@ -534,7 +535,7 @@
         out_shape=(sds(2, NF, NK, 8, NC), sds(NF, NK, NR, NC)),
         in_specs=[VM] * 10,
         out_specs=(VM,) * 2,
-        scratch_shapes=[vm(2, 2, NF, 24, NC), vm(2, 4, 24, NC)] + work,
+        scratch_shapes=[vm(4, 2, NF, 24, NC), vm(2, 4, 24, NC)] + work,
         compiler_params=params(6),
         cost_estimate=cost(2),
         name="edge_rows",

time: 26.7 us -> 24.9 us (0.933)
  Pallas kernels: 12.6 us -> 10.8 us
    pallas_call x1, Pallas kernels: 3.42 us -> 2.33 us  [on_device(): pl.pallas_call(lambda *refs: edge_kernel((SPLIT, NK), *refs), out_shape=(...]
    pallas_call x1, Pallas kernels: 2.05 us -> 1.37 us  [on_device(): pl.pallas_call(pack_rows, out_shape=(sds(MSG, NC), sds(MSG, NC)), in_spec...]
  transfers between devices with their start and end apart: 4 -> 4, of which waited for: 1 -> 1; matrix products, arithmetic and copies ran while one was open for 0% -> 0% of each run, Pallas kernels for 28% -> 26%
where the time goes in v2:
time: 24.9 us; the launch traced here: 24.8 us
  starting transfers between devices  12.6 us (51%)
  Pallas kernels  10.8 us (43%)
  between operations  0.85 us (3%)
  waiting for transfers between devices  0.38 us (2%)
    ppermute x1, starting transfers between devices, on_device(): p2 = lax.ppermute(q2, axes, far)  6.03 us
    pallas_call x1, Pallas kernels, on_device(): pl.pallas_call(lambda *refs: inside_kernel((0, SPLIT), *refs), out_shape=...  4.13 us
    ppermute x1, starting transfers between devices, on_device(): r1 = lax.ppermute(m1, axes, near)  3.34 us
    ppermute x1, starting transfers between devices, on_device(): r2 = lax.ppermute(m2, axes, far)  2.81 us
    pallas_call x1, Pallas kernels, on_device(): pl.pallas_call(lambda *refs: finish(SPLIT, *refs), out_shape=(sds(NK, NR,...  2.39 us
    pallas_call x1, Pallas kernels, on_device(): pl.pallas_call(lambda *refs: edge_kernel((SPLIT, NK), *refs), out_shape=(...  2.33 us
    pallas_call x1, Pallas kernels, on_device(): pl.pallas_call(pack_rows, out_shape=(sds(MSG, NC), sds(MSG, NC)), in_spec...  1.37 us
    pallas_call x1, Pallas kernels, on_device(): pl.pallas_call(pack_columns, out_shape=(sds(16 * NT, NC),) * 2 + (sds(2,...  0.58 us
  transfers between devices with their start and end apart: 4, of which 1 were waited for; matrix products, arithmetic and copies ran while one was open for 0% of the time, Pallas kernels for 26%

profile of v2, /device:TPU:1, one launch (start us, length us, event | category | flops | bytes accessed | tf_op | source)
XLA Modules:
  0.0 24.8 jit_solution(10325214783767969351)
XLA Ops:
  0.6 0.0 copy-start.7
  0.6 0.0 copy-start.6
  0.7 0.0 copy-start.5
  0.7 0.0 copy-start.4
  0.7 0.0 copy-start.3
  0.7 0.0 copy-start.2
  0.7 0.0 copy-start.1
  0.7 0.0 copy-start
  0.7 0.0 copy-start.8
  0.7 0.0 copy-start.9
  0.7 1.4 %pack_rows.1 = (f32[208,128]{1,0:T(8,128)S(1)}, f32[208,128]{1,0:T(8,128)S(1)}) custom-call(f32[16,64,128]{2,1,0:T(8,128)} %refs_1_.3, f32[16,64,128]{2,1,0:T(8,128)} %refs_2_.3, f32[16,64,128]{2,1,0:T(8,128)} %refs_3_.3, f32[16,64,128]{2,1,0:T(8,128)} %refs_4_.3, s32[64,128]{1,0:T(8,128)} %refs_8_.3, f32[64,128]{1,0:T(8,128)} %refs_5_.3, ...), custom_call_target="tpu_custom_call" | custom-call | flops 1000000 | bytes 3000000 | tf_op jit(solution)/shard_map/pack_rows/pallas_call | solution.py:492
  2.1 3.3 %collective-permute-start = (f32[208,128]{1,0:T(8,128)S(1)}, f32[208,128]{1,0:T(8,128)S(1)}, u32[]{:S(2)}, u32[]{:S(2)}) collective-permute-start(f32[208,128]{1,0:T(8,128)S(1)} %get-tuple-element.20), channel_id=1, source_target_pairs={{0,16},{1,17},{2,18},{3,19},{4,20},{5,21},{6,22},{7,23},{8,24},{9,... | collective-permute-start | bytes 319496 | tf_op jit(solution)/shard_map/ppermute | solution.py:509
  5.5 2.8 %collective-permute-start.1 = (f32[208,128]{1,0:T(8,128)S(1)}, f32[208,128]{1,0:T(8,128)S(1)}, u32[]{:S(2)}, u32[]{:S(2)}) collective-permute-start(f32[208,128]{1,0:T(8,128)S(1)} %get-tuple-element.21), channel_id=1, source_target_pairs={{16,32},{17,33},{18,34},{19,35},{20,36},{21,37},{22,38},{23,39},{2... | collective-permute-start | bytes 319496 | tf_op jit(solution)/shard_map/ppermute | solution.py:508
  8.3 0.1 broadcast_in_dim.2.refs_0_
  8.4 4.1 %inside.1 = (f32[4,12,64,128]{3,2,1,0:T(8,128)S(1)}, f32[4,64,128]{2,1,0:T(8,128)S(1)}, f32[4,64,128]{2,1,0:T(8,128)S(1)}, f32[4,64,128]{2,1,0:T(8,128)S(1)}, f32[4,64,128]{2,1,0:T(8,128)S(1)}) custom-call(f32[2,16,128]{2,1,0:T(8,128)S(1)} %broadcast_in_dim.2.refs_0_, f32[16,64,128]{2,1,0:T(8,128)S(1)} %copy-done, f32[16,64,128]{2,1,0:T(8,128)S(1)} %copy-done.1, ...), custom_call_target="tpu_custom_call" | custom-call | flops 4000000 | bytes 12000000 | tf_op jit(solution)/shard_map/inside/pallas_call | solution.py:511
  12.6 0.0 collective-permute-done.r1
  12.6 0.4 %collective-permute-done.1.r2 = f32[208,128]{1,0:T(8,128)S(1)} collective-permute-done((f32[208,128]{1,0:T(8,128)S(1)}, f32[208,128]{1,0:T(8,128)S(1)}, u32[]{:S(2)}, u32[]{:S(2)}) %collective-permute-start.1) | collective-permute-done | bytes 106528 | tf_op jit(solution)/shard_map/ppermute | solution.py:508
  13.0 0.6 %pack_columns.1 = (f32[144,128]{1,0:T(8,128)S(1)}, f32[144,128]{1,0:T(8,128)S(1)}, f32[2,216,128]{2,1,0:T(8,128)S(1)}, f32[4,88,128]{2,1,0:T(8,128)S(1)}, f32[4,...) custom-call(f32[208,128]{1,0:T(8,128)S(1)} %collective-permute-done.r1, ...), custom_call_target="tpu_custom_call" | custom-call | flops 1000000 | bytes 3000000 | tf_op jit(solution)/shard_map/pack_columns/pallas_call | solution.py:521
  13.6 0.5 %collective-permute-start.2 = (f32[144,128]{1,0:T(8,128)S(1)}, f32[144,128]{1,0:T(8,128)S(1)}, u32[]{:S(2)}, u32[]{:S(2)}) collective-permute-start(f32[144,128]{1,0:T(8,128)S(1)} %get-tuple-element.26), channel_id=1, source_target_pairs={{0,1},{1,0},{2,3},{3,2},{4,5},{5,4},{6,7},{7,6},{8,9},{9,8},{10,11... | collective-permute-start | bytes 221192 | tf_op jit(solution)/shard_map/ppermute | solution.py:532
  14.0 6.0 %collective-permute-start.3 = (f32[144,128]{1,0:T(8,128)S(1)}, f32[144,128]{1,0:T(8,128)S(1)}, u32[]{:S(2)}, u32[]{:S(2)}) collective-permute-start(f32[144,128]{1,0:T(8,128)S(1)} %get-tuple-element.27), channel_id=1, source_target_pairs={{0,15},{1,2},{2,1},{3,4},{4,3},{5,6},{6,5},{7,8},{8,7},{9,10},{10,... | collective-permute-start | bytes 221192 | tf_op jit(solution)/shard_map/ppermute | solution.py:531
  20.0 2.3 %edge_rows.1 = (f32[2,4,16,8,128]{4,3,2,1,0:T(8,128)S(1)}, f32[4,16,64,128]{3,2,1,0:T(8,128)S(1)}) custom-call(f32[2,16,128]{2,1,0:T(8,128)S(1)} %broadcast_in_dim.2.refs_0_, f32[16,64,128]{2,1,0:T(8,128)S(1)} %copy-done, f32[16,64,128]{2,1,0:T(8,128)S(1)} %copy-done.1, f32[16,64,128]{2,1,0:T(8,128)S(1)} %copy-done.2, f32[16,64,128]{2,1,0:T(8,128)S(1)} %copy-done.3, ...), custom_call_target="tpu_custom_call" | custom-call | flops 2000000 | bytes 6000000 | tf_op jit(solution)/shard_map/edge_rows/pallas_call | solution.py:533
  22.4 0.0 collective-permute-done.2.refs_1_
  22.4 0.0 collective-permute-done.3.refs_2_
  22.4 2.4 %finish.1 = (f32[16,64,128]{2,1,0:T(8,128)}, f32[16,64,128]{2,1,0:T(8,128)}, f32[16,64,128]{2,1,0:T(8,128)}, f32[16,64,128]{2,1,0:T(8,128)}) custom-call(f32[2,16,128]{2,1,0:T(8,128)S(1)} %broadcast_in_dim.2.refs_0_, f32[144,128]{1,0:T(8,128)S(1)} %collective-permute-done.2.refs_1_, f32[144,128]{1,0:T(8,128)S(1)} %collective-permute-done.3.refs_2_, ...), custom_call_target="tpu_custom_call" | custom-call | flops 2000000 | bytes 6000000 | tf_op jit(solution)/shard_map/finish/pallas_call | solution.py:543
  (11 shorter events, 0.0 us)
Async XLA Ops:
  0.6 7.7 %copy-start.7 = (f32[64,128]{1,0:T(8,128)S(1)}, f32[64,128]{1,0:T(8,128)}, u32[]{:S(2)}) copy-start(f32[64,128]{1,0:T(8,128)} %refs_7_.3) | copy-start | bytes 98308
  0.6 7.7 %copy-start.6 = (f32[64,128]{1,0:T(8,128)S(1)}, f32[64,128]{1,0:T(8,128)}, u32[]{:S(2)}) copy-start(f32[64,128]{1,0:T(8,128)} %refs_6_.3) | copy-start | bytes 98308
  0.7 7.7 %copy-start.5 = (f32[64,128]{1,0:T(8,128)S(1)}, f32[64,128]{1,0:T(8,128)}, u32[]{:S(2)}) copy-start(f32[64,128]{1,0:T(8,128)} %refs_5_.3) | copy-start | bytes 98308
  0.7 7.7 %copy-start.4 = (s32[64,128]{1,0:T(8,128)S(1)}, s32[64,128]{1,0:T(8,128)}, u32[]{:S(2)}) copy-start(s32[64,128]{1,0:T(8,128)} %refs_8_.3) | copy-start | bytes 98308
  0.7 7.7 %copy-start.3 = (f32[16,64,128]{2,1,0:T(8,128)S(1)}, f32[16,64,128]{2,1,0:T(8,128)}, u32[]{:S(2)}) copy-start(f32[16,64,128]{2,1,0:T(8,128)} %refs_4_.3) | copy-start | bytes 1572868
  0.7 7.7 %copy-start.2 = (f32[16,64,128]{2,1,0:T(8,128)S(1)}, f32[16,64,128]{2,1,0:T(8,128)}, u32[]{:S(2)}) copy-start(f32[16,64,128]{2,1,0:T(8,128)} %refs_3_.3) | copy-start | bytes 1572868
  0.7 7.7 %copy-start.1 = (f32[16,64,128]{2,1,0:T(8,128)S(1)}, f32[16,64,128]{2,1,0:T(8,128)}, u32[]{:S(2)}) copy-start(f32[16,64,128]{2,1,0:T(8,128)} %refs_2_.3) | copy-start | bytes 1572868
  0.7 7.7 %copy-start = (f32[16,64,128]{2,1,0:T(8,128)S(1)}, f32[16,64,128]{2,1,0:T(8,128)}, u32[]{:S(2)}) copy-start(f32[16,64,128]{2,1,0:T(8,128)} %refs_1_.3) | copy-start | bytes 1572868
  0.7 7.6 %copy-start.8 = (f32[16]{0:T(128)S(1)}, f32[16]{0:T(128)}, u32[]{:S(2)}) copy-start(f32[16]{0:T(128)} %param.19) | copy-start | bytes 196
  0.7 7.6 %copy-start.9 = (f32[16]{0:T(128)S(1)}, f32[16]{0:T(128)}, u32[]{:S(2)}) copy-start(f32[16]{0:T(128)} %param.18) | copy-start | bytes 196
  2.1 10.5 %collective-permute-start = (f32[208,128]{1,0:T(8,128)S(1)}, f32[208,128]{1,0:T(8,128)S(1)}, u32[]{:S(2)}, u32[]{:S(2)}) collective-permute-start(f32[208,128]{1,0:T(8,128)S(1)} %get-tuple-element.20), channel_id=1, source_target_pairs={{0,16},{1,17},{2,18},{3,19},{4,20},{5,21},{6,22},{7,23},{8,24},{9,... | collective-permute-start | bytes 319496 | tf_op jit(solution)/shard_map/ppermute | solution.py:509
  5.5 7.5 %collective-permute-start.1 = (f32[208,128]{1,0:T(8,128)S(1)}, f32[208,128]{1,0:T(8,128)S(1)}, u32[]{:S(2)}, u32[]{:S(2)}) collective-permute-start(f32[208,128]{1,0:T(8,128)S(1)} %get-tuple-element.21), channel_id=1, source_target_pairs={{16,32},{17,33},{18,34},{19,35},{20,36},{21,37},{22,38},{23,39},{2... | collective-permute-start | bytes 319496 | tf_op jit(solution)/shard_map/ppermute | solution.py:508
  13.6 8.8 %collective-permute-start.2 = (f32[144,128]{1,0:T(8,128)S(1)}, f32[144,128]{1,0:T(8,128)S(1)}, u32[]{:S(2)}, u32[]{:S(2)}) collective-permute-start(f32[144,128]{1,0:T(8,128)S(1)} %get-tuple-element.26), channel_id=1, source_target_pairs={{0,1},{1,0},{2,3},{3,2},{4,5},{5,4},{6,7},{7,6},{8,9},{9,8},{10,11... | collective-permute-start | bytes 221192 | tf_op jit(solution)/shard_map/ppermute | solution.py:532
  14.0 8.4 %collective-permute-start.3 = (f32[144,128]{1,0:T(8,128)S(1)}, f32[144,128]{1,0:T(8,128)S(1)}, u32[]{:S(2)}, u32[]{:S(2)}) collective-permute-start(f32[144,128]{1,0:T(8,128)S(1)} %get-tuple-element.27), channel_id=1, source_target_pairs={{0,15},{1,2},{2,1},{3,4},{4,3},{5,6},{6,5},{7,8},{8,7},{9,10},{10,... | collective-permute-start | bytes 221192 | tf_op jit(solution)/shard_map/ppermute | solution.py:531

commit v3 on v2

--- a/solution.py
+++ b/solution.py
@@ -63,69 +63,66 @@
     return out
 
 
-def pack_rows(t, s, u, v, bat, wd, ht, cor, m1, m2, fl, pn, ibuf, sems):
+def put_rows(dst, tile, planes, r0):
+    for q in range(NF):
+        for k in range(NK):
+            i = (q * NK + k) * HALO
+            dst[i : i + HALO, :] = tile(q, k, r0)
+    for q in range(4):
+        i = NF * NK * HALO + q * HALO
+        dst[i : i + HALO, :] = planes(q, r0)
+    dst[MSG - 4 : MSG, :] = jnp.zeros((4, NC), F32)
+
+
+def pack_rows(t, s, u, v, bat, wd, ht, cor, mt, ms, far, mix, fl, pn, ibuf, tm, sm, sems):
     lat = lax.axis_index("lat")
-    last = lax.axis_size("lat") - 1
-    copies = []
-    for side in (0, 1):
-        rows = pl.ds(side * (NR - 8), 8)
-        for q, x in enumerate((t, s, u, v)):
-            copies.append(
-                pltpu.make_async_copy(x.at[:, rows, :], fl.at[q, side], sems.at[4 * side + q])
-            )
-    for q, x in enumerate((wd, ht, cor)):
-        copies.append(pltpu.make_async_copy(x, pn.at[q], sems.at[8 + q]))
-    copies.append(pltpu.make_async_copy(bat, ibuf, sems.at[11]))
+    odd = lax.rem(lat, 2) == 1
+    last = lat == lax.axis_size("lat") - 1
+    rows = pl.ds(pl.multiple_of(jnp.where(odd, NR - 8, 0), 8), 8)
+    copies = [
+        pltpu.make_async_copy(x.at[:, rows, :], fl.at[q], sems.at[q])
+        for q, x in enumerate((t, s, u, v))
+    ]
+    copies += [
+        pltpu.make_async_copy(x.at[rows, :], pn.at[q], sems.at[NF + q])
+        for q, x in enumerate((wd, ht, cor))
+    ]
+    copies.append(pltpu.make_async_copy(bat.at[rows, :], ibuf, sems.at[NF + 3]))
+    copies.append(pltpu.make_async_copy(mt, tm, sems.at[8]))
+    copies.append(pltpu.make_async_copy(ms, sm, sems.at[9]))
     for c in copies:
         c.start()
-    zero = jnp.zeros((8, NC), F32)
-    m1[MSG - 8 : MSG, :] = zero
-    m2[MSG - 8 : MSG, :] = zero
     for c in copies:
         c.wait()
-    for r in (0, NR - 8):
-        pn[3, r : r + 8, :] = ibuf[r : r + 8, :].astype(F32)
-    base = NF * NK * HALO
-
-    def plain(dst, side):
-        r0 = 0 if side == 0 else NR - HALO
-        for q in range(NF):
-            for k in range(NK):
-                i = (q * NK + k) * HALO
-                dst[i : i + HALO, :] = fl[q, side, k, r0 % 8 : r0 % 8 + HALO, :]
-        for q in range(4):
-            i = base + q * HALO
-            dst[i : i + HALO, :] = pn[q, r0 : r0 + HALO, :]
-
-    def folded(dst):
+    pn[3] = ibuf[...].astype(F32)
+    for k in range(NK):
+        mix[0, k : k + 1, :] = jnp.full((1, NC), tm[k], F32)
+        mix[1, k : k + 1, :] = jnp.full((1, NC), sm[k], F32)
+
+    def plain(r0):
+        put_rows(
+            far, lambda q, k, r: fl[q, k, r : r + HALO, :], lambda q, r: pn[q, r : r + HALO, :], r0
+        )
+
+    @pl.when(jnp.logical_not(odd))
+    def _():
+        plain(0)
+
+    @pl.when(jnp.logical_and(odd, jnp.logical_not(last)))
+    def _():
+        plain(8 - HALO)
+
+    @pl.when(last)
+    def _():
         back = NC - 1 - lanes()
         for q in range(NF + 1):
             for k in range(NK if q < NF else 4):
-                x = fl[q, 1, k, :, :] if q < NF else pn[k, NR - 8 : NR, :]
-                x = pick(x, back)
+                x = pick(fl[q, k] if q < NF else pn[k], back)
                 x = -x if q in (2, 3) else x
                 i = (q * NK + k) * HALO
                 for m in range(HALO):
-                    dst[i + m : i + m + 1, :] = x[7 - m : 8 - m, :]
-
-    odd = lax.rem(lat, 2) == 1
-
-    @pl.when(jnp.logical_not(odd))
-    def _():
-        plain(m2, 0)
-        plain(m1, 1)
-
-    @pl.when(odd)
-    def _():
-        plain(m1, 0)
-
-    @pl.when(jnp.logical_and(odd, lat != last))
-    def _():
-        plain(m2, 1)
-
-    @pl.when(lat == last)
-    def _():
-        folded(m2)
+                    far[i + m : i + m + 1, :] = x[7 - m : 8 - m, :]
+        far[MSG - 4 : MSG, :] = jnp.zeros((4, NC), F32)
 
 
 PAIR = 2
@@ -157,7 +154,7 @@
                     new = advance(c, e, w, n, s, [cf[g, m, rows, :] for m in range(9)])
                     for q in range(NF):
                         if step == STEPS - 1:
-                            out[q, k, rows, :] = new[q]
+                            out[q, k - levels[0], rows, :] = new[q]
                         else:
                             dst[g, q, r : r + 8, :] = new[q]
             src, dst = dst, src
@@ -187,30 +184,95 @@
     return level, west, east
 
 
-def inside_kernel(levels, mix, t, s, u, v, wd, ht, cor, bat, out, gw, ge, pw, pe, met, a, b, cf):
+def messages(tiles, q1, q2, sw, se, spw, spe):
+    even_lon = lax.rem(lax.axis_index("lon"), 2) == 0
+    lane = lanes()
+    level, block = lane // NB, lane % NB
+    first, second = block < HALO, block < 2 * HALO
+    nth = jnp.where(second, 0, level * 2 + block - 6)
+    plane, column = nth // HALO, lax.rem(nth, HALO)
+
+    def emit(dst_e, dst_w):
+        for dst, strip, planes, start in ((dst_e, se, spe, 2), (dst_w, sw, spw, 3)):
+            for i in tiles:
+                rows = slice(OFF - HALO + 8 * i, OFF - HALO + 8 * i + 8)
+                for pair in (0, 1):
+                    x = pltpu.roll(strip[2 * pair, rows, :], NC - start, 1)
+                    y = strip[2 * pair + 1, rows, :]
+                    if start != HALO:
+                        y = pltpu.roll(y, HALO - start, 1)
+                    z = jnp.where(first, x, y)
+                    if pair == 0:
+                        for m in range(4):
+                            take = jnp.logical_and(plane == m, jnp.logical_not(second))
+                            z = jnp.where(take, pick(planes[m, rows, :], start + column), z)
+                    dst[pair * 8 * NT + 8 * i : pair * 8 * NT + 8 * i + 8, :] = z
+
+    @pl.when(even_lon)
+    def _():
+        emit(q1, q2)
+
+    @pl.when(jnp.logical_not(even_lon))
+    def _():
+        emit(q2, q1)
+
+
+def first_kernel(levels, mix, t, s, u, v, wd, ht, cor, bat, near, out, met, a, b, cf):
+    fl, pn = (t, s, u, v), (wd, ht, cor, bat)
+    odd = lax.rem(lax.axis_index("lat"), 2) == 1
+
+    def plain(r0):
+        put_rows(
+            near,
+            lambda q, k, r: fl[q][k, r : r + HALO, :],
+            lambda q, r: pn[q][r : r + HALO, :].astype(F32),
+            r0,
+        )
+
+    @pl.when(odd)
+    def _():
+        plain(0)
+
+    @pl.when(jnp.logical_not(odd))
+    def _():
+        plain(NR - HALO)
+
+    start_interior(pn[:3], met, a, b)
+    interior(levels, fl, bat, mix, met, a, b, cf, out)
+
+
+def inside_kernel(
+    levels, mix, t, s, u, v, wd, ht, cor, bat, out, q1, q2, sw, se, spw, spe, met, a, b, cf
+):
     fl, pn = (t, s, u, v), (wd, ht, cor, bat)
     level, west, east = strip_index()
+    zero = jnp.zeros((8, NC), F32)
+    for strip in (sw, se, spw, spe):
+        for q in range(4):
+            for r in (0, 8, 72, 80):
+                strip[q, r : r + 8, :] = zero
     for j in range(8):
         rows = slice(8 * j, 8 * j + 8)
+        at = slice(OFF + 8 * j, OFF + 8 * j + 8)
         for q in range(NF):
-            xw = xe = jnp.zeros((8, NC), F32)
+            xw = xe = zero
             for k in range(NK):
                 x = fl[q][k, rows, :]
                 here = level == k
                 xw = jnp.where(here, pick(x, west), xw)
                 xe = jnp.where(here, pick(x, east), xe)
-            gw[q, rows, :] = xw
-            ge[q, rows, :] = xe
+            sw[q, at, :] = xw
+            se[q, at, :] = xe
             x = pn[q][rows, :].astype(F32)
-            pw[q, rows, :] = pick(x, west)
-            pe[q, rows, :] = pick(x, east)
+            spw[q, at, :] = pick(x, west)
+            spe[q, at, :] = pick(x, east)
+    messages(range(1, NT - 1), q1, q2, sw, se, spw, spe)
     start_interior(pn[:3], met, a, b)
     interior(levels, fl, bat, mix, met, a, b, cf, out)
 
 
-def pack_columns(r1, r2, gw, ge, pw, pe, q1, q2, gh, sw, se, spw, spe):
+def pack_columns(r1, r2, i1, i2, i3, i4, i5, i6, q1, q2, sw, se, spw, spe, gh):
     odd = lax.rem(lax.axis_index("lat"), 2) == 1
-    even_lon = lax.rem(lax.axis_index("lon"), 2) == 0
     for i in range(MSG // 8):
         rows = slice(8 * i, 8 * i + 8)
         x1, x2 = r1[rows, :], r2[rows, :]
@@ -220,13 +282,6 @@
     gh[0, MSG:GH, :] = zero
     gh[1, MSG:GH, :] = zero
     level, west, east = strip_index()
-    for own, strip in ((gw, sw), (ge, se), (pw, spw), (pe, spe)):
-        for q in range(4):
-            strip[q, 0:8, :] = zero
-            strip[q, 72:80, :] = zero
-            strip[q, 80:88, :] = zero
-            for j in range(8):
-                strip[q, OFF + 8 * j : OFF + 8 * j + 8, :] = own[q, 8 * j : 8 * j + 8, :]
     for side, at in ((0, OFF - HALO), (1, OFF + NR)):
         for q in range(NF):
             xw = xe = zero
@@ -242,35 +297,7 @@
             x = gh[side, i : i + 8, :]
             spw[q, at : at + HALO, :] = pick(x, west)[:HALO, :]
             spe[q, at : at + HALO, :] = pick(x, east)[:HALO, :]
-    lane = lanes()
-    level, block = lane // NB, lane % NB
-    first, second = block < HALO, block < 2 * HALO
-    nth = jnp.where(second, 0, level * 2 + block - 6)
-    plane, column = nth // HALO, lax.rem(nth, HALO)
-
-    def emit(dst_e, dst_w):
-        for dst, strip, planes, start in ((dst_e, se, spe, 2), (dst_w, sw, spw, 3)):
-            for i in range(NT):
-                rows = slice(OFF - HALO + 8 * i, OFF - HALO + 8 * i + 8)
-                for pair in (0, 1):
-                    x = pltpu.roll(strip[2 * pair, rows, :], NC - start, 1)
-                    y = strip[2 * pair + 1, rows, :]
-                    if start != HALO:
-                        y = pltpu.roll(y, HALO - start, 1)
-                    z = jnp.where(first, x, y)
-                    if pair == 0:
-                        for m in range(4):
-                            take = jnp.logical_and(plane == m, jnp.logical_not(second))
-                            z = jnp.where(take, pick(planes[m, rows, :], start + column), z)
-                    dst[pair * 8 * NT + 8 * i : pair * 8 * NT + 8 * i + 8, :] = z
-
-    @pl.when(even_lon)
-    def _():
-        emit(q1, q2)
-
-    @pl.when(jnp.logical_not(even_lon))
-    def _():
-        emit(q2, q1)
+    messages((0, NT - 1), q1, q2, sw, se, spw, spe)
 
 
 def edge_rows(mix, fl, pn, gh, out, win, pwin):
@@ -287,7 +314,7 @@
         met.append(metric(*[pwin[side, i, 8:16, :] for i in range(3)]))
         wets.append(pwin[side, 3, 8:16, :])
         gwets.append(gh[side, base + 3 * HALO : base + 4 * HALO, :])
-    group = 4
+    group = 8
 
     def body(i, carry):
         work, state = [], []
@@ -343,7 +370,7 @@
 
 
 def finish(
-    split, mix, q1, q2, sw, se, spw, spe, rows_new, inner, inner2,
+    mix, q1, q2, sw, se, spw, spe, rows_new, inner0, inner1, inner2,
     ot, os, ou, ov, aw, ae, bw, be, cw, ce, zed, res, sems,
 ):
     even = lax.rem(lax.axis_index("lon"), 2) == 0
@@ -437,7 +464,13 @@
     for g in range(NK // group):
         for q in range(NF):
             for k in range(g * group, (g + 1) * group):
-                src, at = (inner, k) if k < split else (inner2, k)
+                src, at = [
+                    (x, k - lo)
+                    for x, lo, hi in (
+                        (inner0, 0, FIRST), (inner1, FIRST, SPLIT), (inner2, SPLIT, NK)
+                    )
+                    if lo <= k < hi
+                ][0]
                 for j in range(8):
                     rows = slice(8 * j, 8 * j + 8)
                     x = src[q, at, rows, :]
@@ -476,7 +509,8 @@
     return near, far
 
 
-SPLIT = 12
+FIRST = 6
+SPLIT = 8
 
 
 def on_device(t, s, u, v, bat, wd, ht, cor, mt, ms):
@@ -487,63 +521,79 @@
     cost = lambda us: pl.CostEstimate(
         flops=int(us * 1e6), bytes_accessed=int(us * 3e6), transcendentals=0
     )
-    mix = jnp.broadcast_to(jnp.stack([mt, ms])[:, :, None], (2, NK, NC))
-    hbm = [pltpu.with_memory_space_constraint(x, pltpu.HBM) for x in (t, s, u, v, bat, wd, ht, cor)]
-    m1, m2 = pl.pallas_call(
+    hbm = [
+        pltpu.with_memory_space_constraint(x, pltpu.HBM)
+        for x in (t, s, u, v, bat, wd, ht, cor, mt, ms)
+    ]
+    to_far, mix = pl.pallas_call(
         pack_rows,
-        out_shape=(sds(MSG, NC), sds(MSG, NC)),
-        in_specs=[HB] * 8,
+        out_shape=(sds(MSG, NC), sds(2, NK, NC)),
+        in_specs=[HB] * 10,
         out_specs=(VM,) * 2,
         scratch_shapes=[
-            vm(NF, 2, NK, 8, NC),
-            vm(4, NR, NC),
-            pltpu.VMEM((NR, NC), jnp.int32),
-            pltpu.SemaphoreType.DMA((12,)),
+            vm(NF, NK, 8, NC),
+            vm(4, 8, NC),
+            pltpu.VMEM((8, NC), jnp.int32),
+            pltpu.SMEM((NK,), F32),
+            pltpu.SMEM((NK,), F32),
+            pltpu.SemaphoreType.DMA((10,)),
         ],
         compiler_params=params(6),
         cost_estimate=cost(1),
         name="pack_rows",
     )(*hbm)
     near, far = row_pairs(nl, no)
-    r2 = lax.ppermute(m2, axes, far)
-    r1 = lax.ppermute(m1, axes, near)
+    r2 = lax.ppermute(to_far, axes, far)
     work = [vm(6, NR, NC), vm(PAIR, NF, 80, NC), vm(PAIR, NF, 80, NC), vm(PAIR, 9, NR, NC)]
-    inner, gw, ge, pw, pe = pl.pallas_call(
-        lambda *refs: inside_kernel((0, SPLIT), *refs),
-        out_shape=(sds(NF, SPLIT, NR, NC),) + (sds(4, NR, NC),) * 4,
+    to_near, inner0 = pl.pallas_call(
+        lambda *refs: first_kernel((0, FIRST), *refs),
+        out_shape=(sds(MSG, NC), sds(NF, FIRST, NR, NC)),
         in_specs=[VM] * 9,
-        out_specs=(VM,) * 5,
+        out_specs=(VM,) * 2,
+        scratch_shapes=work,
+        compiler_params=params(6),
+        cost_estimate=cost(3),
+        name="first",
+    )(mix, t, s, u, v, wd, ht, cor, bat)
+    r1 = lax.ppermute(to_near, axes, near)
+    strips = (sds(16 * NT, NC),) * 2 + (sds(4, SR, NC),) * 4
+    inner1, *parts = pl.pallas_call(
+        lambda *refs: inside_kernel((FIRST, SPLIT), *refs),
+        out_shape=(sds(NF, SPLIT - FIRST, NR, NC),) + strips,
+        in_specs=[VM] * 9,
+        out_specs=(VM,) * 7,
         scratch_shapes=work,
         compiler_params=params(6),
         cost_estimate=cost(4),
         name="inside",
     )(mix, t, s, u, v, wd, ht, cor, bat)
-    q1, q2, gh, sw, se, spw, spe = pl.pallas_call(
+    q1, q2, sw, se, spw, spe, gh = pl.pallas_call(
         pack_columns,
-        out_shape=(sds(16 * NT, NC),) * 2 + (sds(2, GH, NC),) + (sds(4, SR, NC),) * 4,
-        in_specs=[VM] * 6,
+        out_shape=strips + (sds(2, GH, NC),),
+        in_specs=[VM] * 8,
         out_specs=(VM,) * 7,
+        input_output_aliases={2 + i: i for i in range(6)},
         compiler_params=params(6),
         cost_estimate=cost(1),
         name="pack_columns",
-    )(r1, r2, gw, ge, pw, pe)
+    )(r1, r2, *parts)
     near, far = column_pairs(nl, no)
     p2 = lax.ppermute(q2, axes, far)
     p1 = lax.ppermute(q1, axes, near)
     rows_new, inner2 = pl.pallas_call(
         lambda *refs: edge_kernel((SPLIT, NK), *refs),
-        out_shape=(sds(2, NF, NK, 8, NC), sds(NF, NK, NR, NC)),
+        out_shape=(sds(2, NF, NK, 8, NC), sds(NF, NK - SPLIT, NR, NC)),
         in_specs=[VM] * 10,
         out_specs=(VM,) * 2,
-        scratch_shapes=[vm(4, 2, NF, 24, NC), vm(2, 4, 24, NC)] + work,
+        scratch_shapes=[vm(8, 2, NF, 24, NC), vm(2, 4, 24, NC)] + work,
         compiler_params=params(6),
         cost_estimate=cost(2),
         name="edge_rows",
     )(mix, t, s, u, v, wd, ht, cor, bat, gh)
     return pl.pallas_call(
-        lambda *refs: finish(SPLIT, *refs),
+        finish,
         out_shape=(sds(NK, NR, NC),) * 4,
-        in_specs=[VM] * 10,
+        in_specs=[VM] * 11,
         out_specs=(HB,) * 4,
         scratch_shapes=[vm(NF, SR, NC)] * 4
         + [vm(9, SR, NC)] * 2
@@ -551,7 +601,7 @@
         compiler_params=params(8),
         cost_estimate=cost(2),
         name="finish",
-    )(mix, p1, p2, sw, se, spw, spe, rows_new, inner, inner2)
+    )(mix, p1, p2, sw, se, spw, spe, rows_new, inner0, inner1, inner2)
 
 
 def solution(mesh):

time: 24.9 us -> 24.6 us (0.988)
  starting transfers between devices: 12.6 us -> 13 us
  waiting for transfers between devices: 0.38 us -> 0.01 us
    pallas_call x4 -> x5, Pallas kernels: 8.48 us -> 7.58 us  [the longest x1 2.42 us: on_device(): pl.pallas_call(finish, out_shape=(sds(NK, NR, NC),) * 4, in_specs=[VM] *...]
    pallas_call x1, Pallas kernels: 2.33 us -> 3.05 us  [on_device(): pl.pallas_call(lambda *refs: edge_kernel((SPLIT, NK), *refs), out_shape=(...]
    ppermute x1, starting transfers between devices: 6.03 us -> 6.43 us  [on_device(): p2 = lax.ppermute(q2, axes, far)]
    ppermute x2, waiting for transfers between devices: 0.38 us -> 0.01 us  [the longest x1 0.01 us: on_device(): r2 = lax.ppermute(to_far, axes, far)]
  transfers between devices with their start and end apart: 4 -> 4, of which waited for: 1 -> 0; matrix products, arithmetic and copies ran while one was open for 0% -> 0% of each run, Pallas kernels for 26% -> 26%
where the time goes in v3:
time: 24.6 us; the launch traced here: 24.5 us
  starting transfers between devices  13 us (53%)
  Pallas kernels  10.6 us (43%)
  between operations  0.85 us (3%)
    ppermute x1, starting transfers between devices, on_device(): p2 = lax.ppermute(q2, axes, far)  6.43 us
    ppermute x1, starting transfers between devices, on_device(): r2 = lax.ppermute(to_far, axes, far)  6.04 us
    pallas_call x1, Pallas kernels, on_device(): pl.pallas_call(lambda *refs: edge_kernel((SPLIT, NK), *refs), out_shape=(...  3.05 us
    pallas_call x1, Pallas kernels, on_device(): pl.pallas_call(finish, out_shape=(sds(NK, NR, NC),) * 4, in_specs=[VM] *...  2.42 us
    pallas_call x1, Pallas kernels, on_device(): pl.pallas_call(lambda *refs: inside_kernel((FIRST, SPLIT), *refs), out_sh...  1.9 us
    pallas_call x1, Pallas kernels, on_device(): pl.pallas_call(lambda *refs: first_kernel((0, FIRST), *refs), out_shape=(...  1.53 us
    pallas_call x1, Pallas kernels, on_device(): pl.pallas_call(pack_rows, out_shape=(sds(MSG, NC), sds(2, NK, NC)), in_sp...  1.25 us
  transfers between devices with their start and end apart: 4, of which 0 were waited for; matrix products, arithmetic and copies ran while one was open for 0% of the time, Pallas kernels for 26%

profile of v3, /device:TPU:1, one launch (start us, length us, event | category | flops | bytes accessed | tf_op | source)
XLA Modules:
  0.0 24.5 jit_solution(1691608624571102664)
XLA Ops:
  0.6 0.0 copy-start.7
  0.6 0.0 copy-start.6
  0.7 0.0 copy-start.5
  0.7 0.0 copy-start.4
  0.7 0.0 copy-start.3
  0.7 0.0 copy-start.2
  0.7 0.0 copy-start.1
  0.7 0.0 copy-start
  0.7 1.3 %pack_rows.1 = (f32[208,128]{1,0:T(8,128)S(1)}, f32[2,16,128]{2,1,0:T(8,128)S(1)}) custom-call(f32[16,64,128]{2,1,0:T(8,128)} %refs_1_.5, f32[16,64,128]{2,1,0:T(8,128)} %refs_2_.5, f32[16,64,128]{2,1,0:T(8,128)} %refs_3_.5, f32[16,64,128]{2,1,0:T(8,128)} %refs_4_.5, s32[64,128]{1,0:T(8,128)} %refs_8_.5, f32[64,128]{1,0:T(8,128)} %refs_5_.5, ...), custom_call_target="tpu_custom_call" | custom-call | flops 1000000 | bytes 3000000 | tf_op jit(solution)/shard_map/pack_rows/pallas_call | solution.py:528
  2.0 6.0 %collective-permute-start.1 = (f32[208,128]{1,0:T(8,128)S(1)}, f32[208,128]{1,0:T(8,128)S(1)}, u32[]{:S(2)}, u32[]{:S(2)}) collective-permute-start(f32[208,128]{1,0:T(8,128)S(1)} %get-tuple-element.26), channel_id=1, source_target_pairs={{16,32},{17,33},{18,34},{19,35},{20,36},{21,37},{22,38},{23,39},{2... | collective-permute-start | bytes 319496 | tf_op jit(solution)/shard_map/ppermute | solution.py:546
  8.0 0.0 copy-done.7
  8.0 0.0 copy-done.6
  8.1 1.5 %first.1 = (f32[208,128]{1,0:T(8,128)S(1)}, f32[4,6,64,128]{3,2,1,0:T(8,128)S(1)}) custom-call(f32[2,16,128]{2,1,0:T(8,128)S(1)} %get-tuple-element.24.refs_0_.mix, f32[16,64,128]{2,1,0:T(8,128)S(1)} %copy-done, f32[16,64,128]{2,1,0:T(8,128)S(1)} %copy-done.1, f32[16,64,128]{2,1,0:T(8,128)S(1)} %copy-done.2, f32[16,64,128]{2,1,0:T(8,128)S(1)} %copy-done.3, ...), custom_call_target="tpu_custom_call" | custom-call | flops 3000000 | bytes 9000000 | tf_op jit(solution)/shard_map/first/pallas_call | solution.py:548
  9.6 0.1 collective-permute-start
  9.7 1.9 %inside.1 = (f32[4,2,64,128]{3,2,1,0:T(8,128)S(1)}, f32[144,128]{1,0:T(8,128)S(1)}, f32[144,128]{1,0:T(8,128)S(1)}, f32[4,88,128]{2,1,0:T(8,128)S(1)}, f32[4,88,...) custom-call(f32[2,16,128]{2,1,0:T(8,128)S(1)} %get-tuple-element.24.refs_0_.mix, ...), custom_call_target="tpu_custom_call" | custom-call | flops 4000000 | bytes 12000000 | tf_op jit(solution)/shard_map/inside/pallas_call | solution.py:560
  11.6 0.0 collective-permute-done.1.r2
  11.7 0.0 collective-permute-done.r1
  11.7 0.5 %pack_columns.1 = (f32[144,128]{1,0:T(8,128)S(1)}, f32[144,128]{1,0:T(8,128)S(1)}, f32[4,88,128]{2,1,0:T(8,128)S(1)}, f32[4,88,128]{2,1,0:T(8,128)S(1)}, f32[4,8...) custom-call(f32[208,128]{1,0:T(8,128)S(1)} %collective-permute-done., ...), custom_call_target="tpu_custom_call", output_to_operand_aliasing={{0}: (2, {}), {1}: (3, {}), {2}: (4, {}), {3}: (5, {}), {4}... | custom-call | flops 1000000 | bytes 3000000 | tf_op jit(solution)/shard_map/pack_columns/pallas_call | solution.py:570
  12.2 0.4 %collective-permute-start.2 = (f32[144,128]{1,0:T(8,128)S(1)}, f32[144,128]{1,0:T(8,128)S(1)}, u32[]{:S(2)}, u32[]{:S(2)}) collective-permute-start(f32[144,128]{1,0:T(8,128)S(1)} %get-tuple-element.33), channel_id=1, source_target_pairs={{0,1},{1,0},{2,3},{3,2},{4,5},{5,4},{6,7},{7,6},{8,9},{9,8},{10,11... | collective-permute-start | bytes 221192 | tf_op jit(solution)/shard_map/ppermute | solution.py:582
  12.6 6.4 %collective-permute-start.3 = (f32[144,128]{1,0:T(8,128)S(1)}, f32[144,128]{1,0:T(8,128)S(1)}, u32[]{:S(2)}, u32[]{:S(2)}) collective-permute-start(f32[144,128]{1,0:T(8,128)S(1)} %get-tuple-element.34), channel_id=1, source_target_pairs={{0,15},{1,2},{2,1},{3,4},{4,3},{5,6},{6,5},{7,8},{8,7},{9,10},{10,... | collective-permute-start | bytes 221192 | tf_op jit(solution)/shard_map/ppermute | solution.py:581
  19.0 3.0 %edge_rows.1 = (f32[2,4,16,8,128]{4,3,2,1,0:T(8,128)S(1)}, f32[4,8,64,128]{3,2,1,0:T(8,128)S(1)}) custom-call(f32[2,16,128]{2,1,0:T(8,128)S(1)} %get-tuple-element.24.refs_0_.mix, f32[16,64,128]{2,1,0:T(8,128)S(1)} %copy-done, f32[16,64,128]{2,1,0:T(8,128)S(1)} %copy-done.1, f32[16,64,128]{2,1,0:T(8,128)S(1)} %copy-done.2, f32[16,64,128]{2,1,0:T(8,128)S(1)} %copy-done.3, ...), custom_call_target="tpu_custom_call" | custom-call | flops 2000000 | bytes 6000000 | tf_op jit(solution)/shard_map/edge_rows/pallas_call | solution.py:583
  22.1 0.0 collective-permute-done.2.q1
  22.1 0.0 collective-permute-done.3.q2
  22.1 2.4 %finish.1 = (f32[16,64,128]{2,1,0:T(8,128)}, f32[16,64,128]{2,1,0:T(8,128)}, f32[16,64,128]{2,1,0:T(8,128)}, f32[16,64,128]{2,1,0:T(8,128)}) custom-call(f32[2,16,128]{2,1,0:T(8,128)S(1)} %get-tuple-element.24.refs_0_.mix, f32[144,128]{1,0:T(8,128)S(1)} %collective-permute-done.2.q1, f32[144,128]{1,0:T(8,128)S(1)} %collective-permute-done.3.q2, ...), custom_call_target="tpu_custom_call" | custom-call | flops 2000000 | bytes 6000000 | tf_op jit(solution)/shard_map/finish/pallas_call | solution.py:593
  (6 shorter events, 0.0 us)
Async XLA Ops:
  0.6 7.4 %copy-start.7 = (f32[64,128]{1,0:T(8,128)S(1)}, f32[64,128]{1,0:T(8,128)}, u32[]{:S(2)}) copy-start(f32[64,128]{1,0:T(8,128)} %refs_7_.5) | copy-start | bytes 98308
  0.6 7.4 %copy-start.6 = (f32[64,128]{1,0:T(8,128)S(1)}, f32[64,128]{1,0:T(8,128)}, u32[]{:S(2)}) copy-start(f32[64,128]{1,0:T(8,128)} %refs_6_.5) | copy-start | bytes 98308
  0.7 7.4 %copy-start.5 = (f32[64,128]{1,0:T(8,128)S(1)}, f32[64,128]{1,0:T(8,128)}, u32[]{:S(2)}) copy-start(f32[64,128]{1,0:T(8,128)} %refs_5_.5) | copy-start | bytes 98308
  0.7 7.4 %copy-start.4 = (s32[64,128]{1,0:T(8,128)S(1)}, s32[64,128]{1,0:T(8,128)}, u32[]{:S(2)}) copy-start(s32[64,128]{1,0:T(8,128)} %refs_8_.5) | copy-start | bytes 98308
  0.7 7.4 %copy-start.3 = (f32[16,64,128]{2,1,0:T(8,128)S(1)}, f32[16,64,128]{2,1,0:T(8,128)}, u32[]{:S(2)}) copy-start(f32[16,64,128]{2,1,0:T(8,128)} %refs_4_.5) | copy-start | bytes 1572868
  0.7 7.4 %copy-start.2 = (f32[16,64,128]{2,1,0:T(8,128)S(1)}, f32[16,64,128]{2,1,0:T(8,128)}, u32[]{:S(2)}) copy-start(f32[16,64,128]{2,1,0:T(8,128)} %refs_3_.5) | copy-start | bytes 1572868
  0.7 7.4 %copy-start.1 = (f32[16,64,128]{2,1,0:T(8,128)S(1)}, f32[16,64,128]{2,1,0:T(8,128)}, u32[]{:S(2)}) copy-start(f32[16,64,128]{2,1,0:T(8,128)} %refs_2_.5) | copy-start | bytes 1572868
  0.7 7.4 %copy-start = (f32[16,64,128]{2,1,0:T(8,128)S(1)}, f32[16,64,128]{2,1,0:T(8,128)}, u32[]{:S(2)}) copy-start(f32[16,64,128]{2,1,0:T(8,128)} %refs_1_.5) | copy-start | bytes 1572868
  2.0 9.7 %collective-permute-start.1 = (f32[208,128]{1,0:T(8,128)S(1)}, f32[208,128]{1,0:T(8,128)S(1)}, u32[]{:S(2)}, u32[]{:S(2)}) collective-permute-start(f32[208,128]{1,0:T(8,128)S(1)} %get-tuple-element.26), channel_id=1, source_target_pairs={{16,32},{17,33},{18,34},{19,35},{20,36},{21,37},{22,38},{23,39},{2... | collective-permute-start | bytes 319496 | tf_op jit(solution)/shard_map/ppermute | solution.py:546
  9.6 2.0 %collective-permute-start = (f32[208,128]{1,0:T(8,128)S(1)}, f32[208,128]{1,0:T(8,128)S(1)}, u32[]{:S(2)}, u32[]{:S(2)}) collective-permute-start(f32[208,128]{1,0:T(8,128)S(1)} %get-tuple-element.25), channel_id=1, source_target_pairs={{0,16},{1,17},{2,18},{3,19},{4,20},{5,21},{6,22},{7,23},{8,24},{9,... | collective-permute-start | bytes 319496 | tf_op jit(solution)/shard_map/ppermute | solution.py:558
  12.2 9.9 %collective-permute-start.2 = (f32[144,128]{1,0:T(8,128)S(1)}, f32[144,128]{1,0:T(8,128)S(1)}, u32[]{:S(2)}, u32[]{:S(2)}) collective-permute-start(f32[144,128]{1,0:T(8,128)S(1)} %get-tuple-element.33), channel_id=1, source_target_pairs={{0,1},{1,0},{2,3},{3,2},{4,5},{5,4},{6,7},{7,6},{8,9},{9,8},{10,11... | collective-permute-start | bytes 221192 | tf_op jit(solution)/shard_map/ppermute | solution.py:582
  12.6 9.5 %collective-permute-start.3 = (f32[144,128]{1,0:T(8,128)S(1)}, f32[144,128]{1,0:T(8,128)S(1)}, u32[]{:S(2)}, u32[]{:S(2)}) collective-permute-start(f32[144,128]{1,0:T(8,128)S(1)} %get-tuple-element.34), channel_id=1, source_target_pairs={{0,15},{1,2},{2,1},{3,4},{4,3},{5,6},{6,5},{7,8},{8,7},{9,10},{10,... | collective-permute-start | bytes 221192 | tf_op jit(solution)/shard_map/ppermute | solution.py:581

commit v4 on v3

--- a/solution.py
+++ b/solution.py
@@ -163,13 +163,16 @@
     lax.fori_loop(0, (levels[1] - levels[0]) // PAIR, level, 0)
 
 
-def start_interior(planes, met, a, b):
+def zero_rims(a, b):
     zero = jnp.zeros((8, NC), F32)
     for g in range(PAIR):
         for q in range(NF):
             for x in (a, b):
                 x[g, q, 0:8, :] = zero
                 x[g, q, NR + 8 : NR + 16, :] = zero
+
+
+def set_metric(planes, met):
     for j in range(8):
         rows = slice(8 * j, 8 * j + 8)
         for i, x in enumerate(metric(*[x[rows, :] for x in planes])):
@@ -237,12 +240,13 @@
     def _():
         plain(NR - HALO)
 
-    start_interior(pn[:3], met, a, b)
+    set_metric(pn[:3], met)
+    zero_rims(a, b)
     interior(levels, fl, bat, mix, met, a, b, cf, out)
 
 
 def inside_kernel(
-    levels, mix, t, s, u, v, wd, ht, cor, bat, out, q1, q2, sw, se, spw, spe, met, a, b, cf
+    levels, mix, t, s, u, v, wd, ht, cor, bat, met, out, q1, q2, sw, se, spw, spe, a, b, cf
 ):
     fl, pn = (t, s, u, v), (wd, ht, cor, bat)
     level, west, east = strip_index()
@@ -267,7 +271,7 @@
             spw[q, at, :] = pick(x, west)
             spe[q, at, :] = pick(x, east)
     messages(range(1, NT - 1), q1, q2, sw, se, spw, spe)
-    start_interior(pn[:3], met, a, b)
+    zero_rims(a, b)
     interior(levels, fl, bat, mix, met, a, b, cf, out)
 
 
@@ -314,7 +318,7 @@
         met.append(metric(*[pwin[side, i, 8:16, :] for i in range(3)]))
         wets.append(pwin[side, 3, 8:16, :])
         gwets.append(gh[side, base + 3 * HALO : base + 4 * HALO, :])
-    group = 8
+    group = 16
 
     def body(i, carry):
         work, state = [], []
@@ -360,12 +364,12 @@
 
 
 def edge_kernel(
-    levels, mix, t, s, u, v, wd, ht, cor, bat, gh, out, more, win, pwin, met, a, b, cf
+    levels, mix, t, s, u, v, wd, ht, cor, bat, gh, met, out, more, win, pwin, a, b, cf
 ):
     fl, pn = (t, s, u, v), (wd, ht, cor, bat)
     edge_rows(mix, fl, pn, gh, out, win, pwin)
     if levels[0] < levels[1]:
-        start_interior(pn[:3], met, a, b)
+        zero_rims(a, b)
         interior(levels, fl, bat, mix, met, a, b, cf, more)
 
 
@@ -454,7 +458,7 @@
     row = lax.broadcasted_iota(jnp.int32, (8, NC), 0)
     top, bottom = row < HALO, row >= 8 - HALO
     outs = (ot, os, ou, ov)
-    group = 4
+    group = 8
 
     def copy(q, g):
         return pltpu.make_async_copy(
@@ -544,12 +548,12 @@
     )(*hbm)
     near, far = row_pairs(nl, no)
     r2 = lax.ppermute(to_far, axes, far)
-    work = [vm(6, NR, NC), vm(PAIR, NF, 80, NC), vm(PAIR, NF, 80, NC), vm(PAIR, 9, NR, NC)]
-    to_near, inner0 = pl.pallas_call(
+    work = [vm(PAIR, NF, 80, NC), vm(PAIR, NF, 80, NC), vm(PAIR, 9, NR, NC)]
+    to_near, inner0, met = pl.pallas_call(
         lambda *refs: first_kernel((0, FIRST), *refs),
-        out_shape=(sds(MSG, NC), sds(NF, FIRST, NR, NC)),
+        out_shape=(sds(MSG, NC), sds(NF, FIRST, NR, NC), sds(6, NR, NC)),
         in_specs=[VM] * 9,
-        out_specs=(VM,) * 2,
+        out_specs=(VM,) * 3,
         scratch_shapes=work,
         compiler_params=params(6),
         cost_estimate=cost(3),
@@ -560,13 +564,13 @@
     inner1, *parts = pl.pallas_call(
         lambda *refs: inside_kernel((FIRST, SPLIT), *refs),
         out_shape=(sds(NF, SPLIT - FIRST, NR, NC),) + strips,
-        in_specs=[VM] * 9,
+        in_specs=[VM] * 10,
         out_specs=(VM,) * 7,
         scratch_shapes=work,
         compiler_params=params(6),
         cost_estimate=cost(4),
         name="inside",
-    )(mix, t, s, u, v, wd, ht, cor, bat)
+    )(mix, t, s, u, v, wd, ht, cor, bat, met)
     q1, q2, sw, se, spw, spe, gh = pl.pallas_call(
         pack_columns,
         out_shape=strips + (sds(2, GH, NC),),
@@ -583,13 +587,13 @@
     rows_new, inner2 = pl.pallas_call(
         lambda *refs: edge_kernel((SPLIT, NK), *refs),
         out_shape=(sds(2, NF, NK, 8, NC), sds(NF, NK - SPLIT, NR, NC)),
-        in_specs=[VM] * 10,
+        in_specs=[VM] * 11,
         out_specs=(VM,) * 2,
-        scratch_shapes=[vm(8, 2, NF, 24, NC), vm(2, 4, 24, NC)] + work,
+        scratch_shapes=[vm(16, 2, NF, 24, NC), vm(2, 4, 24, NC)] + work,
         compiler_params=params(6),
         cost_estimate=cost(2),
         name="edge_rows",
-    )(mix, t, s, u, v, wd, ht, cor, bat, gh)
+    )(mix, t, s, u, v, wd, ht, cor, bat, gh, met)
     return pl.pallas_call(
         finish,
         out_shape=(sds(NK, NR, NC),) * 4,
@@ -597,7 +601,7 @@
         out_specs=(HB,) * 4,
         scratch_shapes=[vm(NF, SR, NC)] * 4
         + [vm(9, SR, NC)] * 2
-        + [vm(NF, NR, NC), vm(NF, NK, NR, NC), pltpu.SemaphoreType.DMA((NF, 4))],
+        + [vm(NF, NR, NC), vm(NF, NK, NR, NC), pltpu.SemaphoreType.DMA((NF, 2))],
         compiler_params=params(8),
         cost_estimate=cost(2),
         name="finish",

time: 24.6 us -> 24.5 us (level)
  no operation moved by 1% of the time
where the time goes in v4:
time: 24.5 us; the launch traced here: 24.4 us
  starting transfers between devices  13 us (53%)
  Pallas kernels  10.5 us (43%)
  between operations  0.85 us (3%)
    ppermute x1, starting transfers between devices, on_device(): p2 = lax.ppermute(q2, axes, far)  6.43 us
    ppermute x1, starting transfers between devices, on_device(): r2 = lax.ppermute(to_far, axes, far)  6.04 us
    pallas_call x1, Pallas kernels, on_device(): pl.pallas_call(lambda *refs: edge_kernel((SPLIT, NK), *refs), out_shape=(...  2.95 us
    pallas_call x1, Pallas kernels, on_device(): pl.pallas_call(finish, out_shape=(sds(NK, NR, NC),) * 4, in_specs=[VM] *...  2.38 us
    pallas_call x1, Pallas kernels, on_device(): pl.pallas_call(lambda *refs: inside_kernel((FIRST, SPLIT), *refs), out_sh...  1.89 us
    pallas_call x1, Pallas kernels, on_device(): pl.pallas_call(lambda *refs: first_kernel((0, FIRST), *refs), out_shape=(...  1.53 us
    pallas_call x1, Pallas kernels, on_device(): pl.pallas_call(pack_rows, out_shape=(sds(MSG, NC), sds(2, NK, NC)), in_sp...  1.25 us
  transfers between devices with their start and end apart: 4, of which 0 were waited for; matrix products, arithmetic and copies ran while one was open for 0% of the time, Pallas kernels for 26%

profile of v4, /device:TPU:1, one launch (start us, length us, event | category | flops | bytes accessed | tf_op | source)
XLA Modules:
  0.0 24.4 jit_solution(13383615455676389847)
XLA Ops:
  0.6 0.0 copy-start.7
  0.6 0.0 copy-start.6
  0.7 0.0 copy-start.5
  0.7 0.0 copy-start.4
  0.7 0.0 copy-start.3
  0.7 0.0 copy-start.2
  0.7 0.0 copy-start.1
  0.7 0.0 copy-start
  0.7 1.3 %pack_rows.1 = (f32[208,128]{1,0:T(8,128)S(1)}, f32[2,16,128]{2,1,0:T(8,128)S(1)}) custom-call(f32[16,64,128]{2,1,0:T(8,128)} %refs_1_.5, f32[16,64,128]{2,1,0:T(8,128)} %refs_2_.5, f32[16,64,128]{2,1,0:T(8,128)} %refs_3_.5, f32[16,64,128]{2,1,0:T(8,128)} %refs_4_.5, s32[64,128]{1,0:T(8,128)} %refs_8_.5, f32[64,128]{1,0:T(8,128)} %refs_5_.5, ...), custom_call_target="tpu_custom_call" | custom-call | flops 1000000 | bytes 3000000 | tf_op jit(solution)/shard_map/pack_rows/pallas_call | solution.py:532
  2.0 6.0 %collective-permute-start.1 = (f32[208,128]{1,0:T(8,128)S(1)}, f32[208,128]{1,0:T(8,128)S(1)}, u32[]{:S(2)}, u32[]{:S(2)}) collective-permute-start(f32[208,128]{1,0:T(8,128)S(1)} %get-tuple-element.27), channel_id=1, source_target_pairs={{16,32},{17,33},{18,34},{19,35},{20,36},{21,37},{22,38},{23,39},{2... | collective-permute-start | bytes 319496 | tf_op jit(solution)/shard_map/ppermute | solution.py:550
  8.0 0.0 copy-done.7
  8.0 0.0 copy-done.6
  8.1 1.5 %first.1 = (f32[208,128]{1,0:T(8,128)S(1)}, f32[4,6,64,128]{3,2,1,0:T(8,128)S(1)}, f32[6,64,128]{2,1,0:T(8,128)S(1)}) custom-call(f32[2,16,128]{2,1,0:T(8,128)S(1)} %get-tuple-element.25.refs_0_.mix, f32[16,64,128]{2,1,0:T(8,128)S(1)} %copy-done, f32[16,64,128]{2,1,0:T(8,128)S(1)} %copy-done.1, f32[16,64,128]{2,1,0:T(8,128)S(1)} %copy-done.2, ...), custom_call_target="tpu_custom_call" | custom-call | flops 3000000 | bytes 9000000 | tf_op jit(solution)/shard_map/first/pallas_call | solution.py:552
  9.6 0.1 collective-permute-start
  9.7 1.9 %inside.1 = (f32[4,2,64,128]{3,2,1,0:T(8,128)S(1)}, f32[144,128]{1,0:T(8,128)S(1)}, f32[144,128]{1,0:T(8,128)S(1)}, f32[4,88,128]{2,1,0:T(8,128)S(1)}, f32[4,88,...) custom-call(f32[2,16,128]{2,1,0:T(8,128)S(1)} %get-tuple-element.25.refs_0_.mix, ...), custom_call_target="tpu_custom_call" | custom-call | flops 4000000 | bytes 12000000 | tf_op jit(solution)/shard_map/inside/pallas_call | solution.py:564
  11.6 0.0 collective-permute-done.1.r2
  11.6 0.0 collective-permute-done.r1
  11.7 0.5 %pack_columns.1 = (f32[144,128]{1,0:T(8,128)S(1)}, f32[144,128]{1,0:T(8,128)S(1)}, f32[4,88,128]{2,1,0:T(8,128)S(1)}, f32[4,88,128]{2,1,0:T(8,128)S(1)}, f32[4,8...) custom-call(f32[208,128]{1,0:T(8,128)S(1)} %collective-permute-done., ...), custom_call_target="tpu_custom_call", output_to_operand_aliasing={{0}: (2, {}), {1}: (3, {}), {2}: (4, {}), {3}: (5, {}), {4}... | custom-call | flops 1000000 | bytes 3000000 | tf_op jit(solution)/shard_map/pack_columns/pallas_call | solution.py:574
  12.2 0.4 %collective-permute-start.2 = (f32[144,128]{1,0:T(8,128)S(1)}, f32[144,128]{1,0:T(8,128)S(1)}, u32[]{:S(2)}, u32[]{:S(2)}) collective-permute-start(f32[144,128]{1,0:T(8,128)S(1)} %get-tuple-element.35), channel_id=1, source_target_pairs={{0,1},{1,0},{2,3},{3,2},{4,5},{5,4},{6,7},{7,6},{8,9},{9,8},{10,11... | collective-permute-start | bytes 221192 | tf_op jit(solution)/shard_map/ppermute | solution.py:586
  12.6 6.4 %collective-permute-start.3 = (f32[144,128]{1,0:T(8,128)S(1)}, f32[144,128]{1,0:T(8,128)S(1)}, u32[]{:S(2)}, u32[]{:S(2)}) collective-permute-start(f32[144,128]{1,0:T(8,128)S(1)} %get-tuple-element.36), channel_id=1, source_target_pairs={{0,15},{1,2},{2,1},{3,4},{4,3},{5,6},{6,5},{7,8},{8,7},{9,10},{10,... | collective-permute-start | bytes 221192 | tf_op jit(solution)/shard_map/ppermute | solution.py:585
  19.0 3.0 %edge_rows.1 = (f32[2,4,16,8,128]{4,3,2,1,0:T(8,128)S(1)}, f32[4,8,64,128]{3,2,1,0:T(8,128)S(1)}) custom-call(f32[2,16,128]{2,1,0:T(8,128)S(1)} %get-tuple-element.25.refs_0_.mix, f32[16,64,128]{2,1,0:T(8,128)S(1)} %copy-done, f32[16,64,128]{2,1,0:T(8,128)S(1)} %copy-done.1, f32[16,64,128]{2,1,0:T(8,128)S(1)} %copy-done.2, f32[16,64,128]{2,1,0:T(8,128)S(1)} %copy-done.3, ...), custom_call_target="tpu_custom_call" | custom-call | flops 2000000 | bytes 6000000 | tf_op jit(solution)/shard_map/edge_rows/pallas_call | solution.py:587
  22.0 0.0 collective-permute-done.2.q1
  22.0 0.0 collective-permute-done.3.q2
  22.0 2.4 %finish.1 = (f32[16,64,128]{2,1,0:T(8,128)}, f32[16,64,128]{2,1,0:T(8,128)}, f32[16,64,128]{2,1,0:T(8,128)}, f32[16,64,128]{2,1,0:T(8,128)}) custom-call(f32[2,16,128]{2,1,0:T(8,128)S(1)} %get-tuple-element.25.refs_0_.mix, f32[144,128]{1,0:T(8,128)S(1)} %collective-permute-done.2.q1, f32[144,128]{1,0:T(8,128)S(1)} %collective-permute-done.3.q2, ...), custom_call_target="tpu_custom_call" | custom-call | flops 2000000 | bytes 6000000 | tf_op jit(solution)/shard_map/finish/pallas_call | solution.py:597
  (6 shorter events, 0.0 us)
Async XLA Ops:
  0.6 7.4 %copy-start.7 = (f32[64,128]{1,0:T(8,128)S(1)}, f32[64,128]{1,0:T(8,128)}, u32[]{:S(2)}) copy-start(f32[64,128]{1,0:T(8,128)} %refs_7_.5) | copy-start | bytes 98308
  0.6 7.4 %copy-start.6 = (f32[64,128]{1,0:T(8,128)S(1)}, f32[64,128]{1,0:T(8,128)}, u32[]{:S(2)}) copy-start(f32[64,128]{1,0:T(8,128)} %refs_6_.5) | copy-start | bytes 98308
  0.7 7.4 %copy-start.5 = (f32[64,128]{1,0:T(8,128)S(1)}, f32[64,128]{1,0:T(8,128)}, u32[]{:S(2)}) copy-start(f32[64,128]{1,0:T(8,128)} %refs_5_.5) | copy-start | bytes 98308
  0.7 7.4 %copy-start.4 = (s32[64,128]{1,0:T(8,128)S(1)}, s32[64,128]{1,0:T(8,128)}, u32[]{:S(2)}) copy-start(s32[64,128]{1,0:T(8,128)} %refs_8_.5) | copy-start | bytes 98308
  0.7 7.4 %copy-start.3 = (f32[16,64,128]{2,1,0:T(8,128)S(1)}, f32[16,64,128]{2,1,0:T(8,128)}, u32[]{:S(2)}) copy-start(f32[16,64,128]{2,1,0:T(8,128)} %refs_4_.5) | copy-start | bytes 1572868
  0.7 7.4 %copy-start.2 = (f32[16,64,128]{2,1,0:T(8,128)S(1)}, f32[16,64,128]{2,1,0:T(8,128)}, u32[]{:S(2)}) copy-start(f32[16,64,128]{2,1,0:T(8,128)} %refs_3_.5) | copy-start | bytes 1572868
  0.7 7.4 %copy-start.1 = (f32[16,64,128]{2,1,0:T(8,128)S(1)}, f32[16,64,128]{2,1,0:T(8,128)}, u32[]{:S(2)}) copy-start(f32[16,64,128]{2,1,0:T(8,128)} %refs_2_.5) | copy-start | bytes 1572868
  0.7 7.4 %copy-start = (f32[16,64,128]{2,1,0:T(8,128)S(1)}, f32[16,64,128]{2,1,0:T(8,128)}, u32[]{:S(2)}) copy-start(f32[16,64,128]{2,1,0:T(8,128)} %refs_1_.5) | copy-start | bytes 1572868
  2.0 9.7 %collective-permute-start.1 = (f32[208,128]{1,0:T(8,128)S(1)}, f32[208,128]{1,0:T(8,128)S(1)}, u32[]{:S(2)}, u32[]{:S(2)}) collective-permute-start(f32[208,128]{1,0:T(8,128)S(1)} %get-tuple-element.27), channel_id=1, source_target_pairs={{16,32},{17,33},{18,34},{19,35},{20,36},{21,37},{22,38},{23,39},{2... | collective-permute-start | bytes 319496 | tf_op jit(solution)/shard_map/ppermute | solution.py:550
  9.6 2.0 %collective-permute-start = (f32[208,128]{1,0:T(8,128)S(1)}, f32[208,128]{1,0:T(8,128)S(1)}, u32[]{:S(2)}, u32[]{:S(2)}) collective-permute-start(f32[208,128]{1,0:T(8,128)S(1)} %get-tuple-element.26), channel_id=1, source_target_pairs={{0,16},{1,17},{2,18},{3,19},{4,20},{5,21},{6,22},{7,23},{8,24},{9,... | collective-permute-start | bytes 319496 | tf_op jit(solution)/shard_map/ppermute | solution.py:562
  12.2 9.8 %collective-permute-start.2 = (f32[144,128]{1,0:T(8,128)S(1)}, f32[144,128]{1,0:T(8,128)S(1)}, u32[]{:S(2)}, u32[]{:S(2)}) collective-permute-start(f32[144,128]{1,0:T(8,128)S(1)} %get-tuple-element.35), channel_id=1, source_target_pairs={{0,1},{1,0},{2,3},{3,2},{4,5},{5,4},{6,7},{7,6},{8,9},{9,8},{10,11... | collective-permute-start | bytes 221192 | tf_op jit(solution)/shard_map/ppermute | solution.py:586
  12.6 9.4 %collective-permute-start.3 = (f32[144,128]{1,0:T(8,128)S(1)}, f32[144,128]{1,0:T(8,128)S(1)}, u32[]{:S(2)}, u32[]{:S(2)}) collective-permute-start(f32[144,128]{1,0:T(8,128)S(1)} %get-tuple-element.36), channel_id=1, source_target_pairs={{0,15},{1,2},{2,1},{3,4},{4,3},{5,6},{6,5},{7,8},{8,7},{9,10},{10,... | collective-permute-start | bytes 221192 | tf_op jit(solution)/shard_map/ppermute | solution.py:585
